TPU v7x, 512 devices: a whole 4x8x8 slice. The times are simulated.
512 devices in a mesh: frame: 128 (over x, y_hi, z), head: 4 (over y_lo, core).
Axes of the slice: x: 4, y: 8 (y_hi: 4, y_lo: 2; y = y_hi * 2 + y_lo), z: 8, core: 2. Of those that a mesh axis runs over, the one named last changes fastest.
Arguments:
- encoded: bfloat16 [262144, 1152], P(('frame', 'head')), may hold values from -32 to 32
- block_source: int32 [512, 1], P('frame'), may hold values from 0 to 3; in each aligned block of 4 rows (0 to 3, 4 to 7, ...) at most 2 rows name the same one
- block_slot: int32 [128, 4, 4], P('frame'), may hold values from 0 to 3, each once within a row
- video_patches: int32 [3], replicated, may hold values from 1 to 32768, 65536 in all
- latent_video: int32 [384], replicated, may hold values from 0 to 2, as said below
- media_gain: float32 [1152], replicated, may hold values from 0.5 to 1.5
- queries: bfloat16 [768, 4096], P('frame', 'head'), may hold values from -160 to 160
- w_key: bfloat16 [1152, 4096], P('frame', 'head'), may hold values from -0.1875 to 0.1875
- w_value: bfloat16 [1152, 4096], P('frame', 'head'), may hold values from -0.1875 to 0.1875
Outputs:
- attended: bfloat16 [768, 4096], P('frame', 'head')
Inputs may be any that keep to these rules, and one draw needn't show every extreme that they name: `block_source`: within the 4 blocks of one frame shard no source is named more than 2 times. Each row block_slot[f, s, :] holds every offset once. `video_patches`: the counts sum to 65536. `latent_video`: every video owns exactly 256 latents.
All inputs are finite; a program needn't handle non-finite values.
Results may differ from a plain program's by a relative error of at most 0.011.
Values may be sent and summed in bfloat16 or wider, within the bound.
No kernel may reach another device: no remote copies, remote signals or barrier semaphores. Data moves between devices by JAX's collectives and lax.ppermute only.
A program may use at most 64 MiB of HBM per device.

v0:
```python
import jax
import jax.numpy as jnp
from jax import lax
from jax.sharding import PartitionSpec as P

HEAD_DIM = 128
LAT_BLK = 2
BLK_ROWS = 128
NB = 4


def layer_norm(rows, media_gain):
    values = rows.astype(jnp.float32)
    center = values - jnp.mean(values, axis=1, keepdims=True)
    spread = jnp.mean(center * center, axis=1, keepdims=True)
    return (center * lax.rsqrt(spread + 1e-06) * media_gain).astype(jnp.bfloat16)


def score_block(query_rows, key_heads, keep, scale):
    heads_here = key_heads.shape[1]
    query_heads = query_rows.reshape(query_rows.shape[0], heads_here, HEAD_DIM)
    scores = (
        jnp.einsum("lhd,phd->hlp", query_heads, key_heads, preferred_element_type=jnp.float32)
        * scale
    )
    return jnp.where(keep[None], scores, -1e30)


def sum_block(masked, head_top, keep, value_heads):
    weights = jnp.where(keep[None], jnp.exp(masked - head_top[:, :, None]), 0.0)
    numer = jnp.einsum(
        "hlp,phd->hld",
        weights.astype(jnp.bfloat16),
        value_heads,
        preferred_element_type=jnp.float32,
    )
    return (numer, jnp.sum(weights, axis=2))


def largest_scores(masked):
    return lax.pmax(jnp.max(masked, axis=2), "frame")


def shards(
    encoded,
    block_source,
    block_slot,
    video_patches,
    latent_video,
    media_gain,
    queries,
    w_key,
    w_value,
):
    source = block_source[:, 0]
    count = source.shape[0]
    earlier = jnp.arange(count)[None, :] < jnp.arange(count)[:, None]
    ranked = jnp.sum(((source[:, None] == source[None, :]) & earlier).astype(jnp.int32), axis=1)
    media = encoded.shape[1]
    blocks_held = encoded.reshape(NB, BLK_ROWS, media)
    every = lax.all_gather(blocks_held, "head", axis=0, tiled=True)
    offset = block_slot[0][source, ranked]
    picked = every[source * NB + offset]
    patches = picked.reshape(count * BLK_ROWS, media)
    normed = layer_norm(patches, media_gain)
    key_rows, value_rows = (
        lax.all_gather(w_key, "frame", axis=0, tiled=True),
        lax.all_gather(w_value, "frame", axis=0, tiled=True),
    )
    keys = jnp.dot(normed, key_rows, preferred_element_type=jnp.float32).astype(jnp.bfloat16)
    values = jnp.dot(normed, value_rows, preferred_element_type=jnp.float32).astype(jnp.bfloat16)
    rows_here = patches.shape[0]
    heads_here = queries.shape[1] // HEAD_DIM
    key_heads = keys.reshape(rows_here, heads_here, HEAD_DIM)
    value_heads = values.reshape(rows_here, heads_here, HEAD_DIM)
    position = lax.axis_index("frame") * rows_here + jnp.arange(rows_here, dtype=jnp.int32)
    bounds = jnp.cumsum(video_patches)
    patch_video = jnp.sum((position[:, None] >= bounds[None, :]).astype(jnp.int32), axis=1)
    every_query = lax.all_gather(queries, "frame", axis=0, tiled=True)
    latent_rows = every_query.shape[0]
    row_video = jnp.repeat(latent_video, LAT_BLK)
    scale = HEAD_DIM ** (-0.5)
    allowed = row_video[:, None] == patch_video[None, :]
    masked = score_block(every_query, key_heads, allowed, scale)
    top = largest_scores(masked)
    numer, total = sum_block(masked, top, allowed, value_heads)
    share = latent_rows // lax.axis_size("frame")
    numer_part, total_part = (
        lax.psum_scatter(numer, "frame", scatter_dimension=1, tiled=True),
        lax.psum_scatter(total, "frame", scatter_dimension=1, tiled=True),
    )
    attended = (numer_part / total_part[:, :, None]).astype(jnp.bfloat16)
    return jnp.transpose(attended, (1, 0, 2)).reshape(share, heads_here * HEAD_DIM)


def solution(mesh):
    placed = (
        P(("frame", "head"), None),
        P("frame", None),
        P("frame", None, None),
        P(),
        P(),
        P(),
        P("frame", "head"),
        P("frame", "head"),
        P("frame", "head"),
    )
    return jax.shard_map(
        shards, mesh=mesh, in_specs=placed, out_specs=P("frame", "head"), check_vma=False
    )
```

profile of v0, /device:TPU:2, one launch (start us, length us, event | category | flops | bytes accessed | tf_op | source)
XLA Modules:
  0.0 2060.7 jit_solution(4701761987141092587)
XLA Ops:
  6.5 0.0 copy-start
  6.5 0.0 all-gather.12.cloned.1.call-start
  6.5 0.7 all-gather.12.cloned.1.call-update
  7.3 0.0 all-gather.10.cloned.1.call-start
  7.3 0.7 all-gather.10.cloned.1.call-update
  8.0 0.0 all-gather.14.cloned.1.call-start
  8.1 0.7 all-gather.14.cloned.1.call-update
  8.7 0.0 all-gather.8.cloned.1.call-start
  8.8 0.5 all-gather.8.cloned.1.call-update
  9.3 0.0 reduce-scatter.3.cloned.1.call-start
  9.4 0.8 broadcast_in_dim.16
  10.2 0.1 eq.34
  10.3 0.8 reduce-window.8
  11.1 0.9 convert_reduce_fusion.2
  12.1 0.7 fusion.25
  12.7 0.0 copy-done
  12.7 0.6 gather_fusion
  13.4 0.7 fusion.24
  14.0 0.1 convert_reduce_fusion.1
  14.1 1.0 broadcast_compare_fusion
  15.2 125.1 %all-gather.12.cloned.1.call-done = bf16[128,6,1024]{2,1,0:T(8,128)(2,1)} async-done(((bf16[1,6,1024]{2,1,0:T(8,128)(2,1)}), bf16[128,6,1024]{2,1,0:T(8,128)(2,1)}) %all-gather.12.cloned.1.call-update) | async-done | bytes 1572880 | tf_op jit(solution)/shard_map/all_gather | solution.py:79
  140.2 4.4 reshape.130
  144.6 126.0 %all-gather.10.cloned.1.call-done = bf16[128,9,1024]{2,1,0:T(8,128)(2,1)} async-done(((bf16[1,9,1024]{2,1,0:T(8,128)(2,1)}), bf16[128,9,1024]{2,1,0:T(8,128)(2,1)}) %all-gather.10.cloned.1.call-update) | async-done | bytes 2359312 | tf_op jit(solution)/shard_map/all_gather | solution.py:67
  270.6 4.2 reshape.149
  274.8 126.6 %all-gather.14.cloned.1.call-done = bf16[128,9,1024]{2,1,0:T(8,128)(2,1)} async-done(((bf16[1,9,1024]{2,1,0:T(8,128)(2,1)}), bf16[128,9,1024]{2,1,0:T(8,128)(2,1)}) %all-gather.14.cloned.1.call-update) | async-done | bytes 2359312 | tf_op jit(solution)/shard_map/all_gather | solution.py:68
  401.4 5.5 reshape.153
  407.0 0.0 copy-start.4
  407.0 48.8 %all-gather.8.cloned.1.call-done = bf16[16,128,1152]{2,1,0:T(8,128)(2,1)} async-done(((bf16[4,128,1152]{2,1,0:T(8,128)(2,1)}), bf16[16,128,1152]{2,1,0:T(8,128)(2,1)}) %all-gather.8.cloned.1.call-update) | async-done | bytes 4718608 | tf_op jit(solution)/shard_map/all_gather | solution.py:61
  455.8 3.1 gather_fusion.1
  458.9 0.0 copy-start.1
  458.9 0.2 convert_reduce_fusion
  459.1 0.4 multiply_reduce_fusion
  459.6 0.0 copy-done.4
  459.6 0.4 fusion.8
  460.0 0.5 copy-done.1
  460.5 2.6 fusion.12
  463.1 0.0 copy-start.2
  463.1 0.0 copy-start.3
  463.1 1.6 fusion.11
  464.7 0.0 copy-done.2
  464.7 0.0 copy-done.3
  464.7 0.0 copy-start.5
  464.7 6.0 fusion
  470.7 668.0 %pmax.7 = f32[8,768]{1,0:T(8,128)S(1)} all-reduce(f32[8,768]{1,0:T(8,128)S(1)} %get-tuple-element.7), channel_id=1, replica_groups=mesh['frame'=128,'head'=4] {'frame'}, use_global_device_ids=true, to_apply=%region_6.7 | all-reduce | flops 6144 | bytes 49152 | tf_op jit(solution)/shard_map/pmax | solution.py:41
  1138.7 0.0 copy-done.5
  1138.7 7.2 fusion.3
  1145.9 3.5 copy.27
  1149.4 0.0 reduce-scatter.3.cloned.1.call-update
  1149.4 1.3 dynamic-slice
  1151.3 6.5 fusion.1
  1157.8 727.2 %all-reduce = f32[8,768]{1,0:T(8,128)S(1)} all-reduce(f32[8,768]{1,0:T(8,128)S(1)} %fusion.1), channel_id=3, replica_groups=mesh['frame'=128,'head'=4] {'frame'}, use_global_device_ids=true, to_apply=%region_9.10.clone | all-reduce | flops 6144 | bytes 49152
  1885.0 0.1 constant_dynamic-slice_fusion
  1885.1 0.1 copy.28
  1885.2 167.5 %reduce-scatter.3.cloned.1.call-done = f32[8,6,128]{2,0,1:T(8,128)} async-done(((f32[8,768,128]{2,0,1:T(8,128)}), f32[8,6,128]{2,0,1:T(8,128)}) %reduce-scatter.3.cloned.1.call-update) | async-done | bytes 24592 | tf_op jit(solution)/shard_map/reduce_scatter | solution.py:89
  2052.7 0.8 fusion.17
  2053.5 0.6 copy.50
  (4 shorter events, 0.0 us)
Async XLA Ops:
  6.5 6.2 copy-start
  6.5 133.7 %all-gather.12.cloned.1.call-start = ((), (), s32[]{:S(2)}) async-start(), calls=%async_computation.4 | async-start | bytes 2113536 | tf_op jit(solution)/shard_map/all_gather | solution.py:79
  7.3 263.4 %all-gather.10.cloned.1.call-start = ((), (), s32[]{:S(2)}) async-start(), calls=%async_computation.3 | async-start | bytes 4227072 | tf_op jit(solution)/shard_map/all_gather | solution.py:67
  8.0 393.4 %all-gather.14.cloned.1.call-start = ((), (), s32[]{:S(2)}) async-start(), calls=%async_computation.5 | async-start | bytes 4227072 | tf_op jit(solution)/shard_map/all_gather | solution.py:68
  8.7 447.0 %all-gather.8.cloned.1.call-start = ((), (), s32[]{:S(2)}) async-start(), calls=%async_computation.1 | async-start | bytes 5898240 | tf_op jit(solution)/shard_map/all_gather | solution.py:61
  9.3 2043.4 %reduce-scatter.3.cloned.1.call-start = ((), (), s32[]{:S(2)}) async-start(), calls=%async_computation.2 | async-start | bytes 3170304 | tf_op jit(solution)/shard_map/reduce_scatter | solution.py:89
  407.0 52.6 %copy-start.4 = (f32[1152]{0:T(1024)S(1)}, f32[1152]{0:T(1024)}, u32[]{:S(2)}) copy-start(f32[1152]{0:T(1024)} %param.14) | copy-start | bytes 13828
  458.9 1.7 copy-start.1
  463.1 1.6 copy-start.2
  463.1 1.6 copy-start.3
  464.7 674.0 %copy-start.5 = (bf16[64,8,8,128]{3,2,1,0:T(8,128)(2,1)S(1)}, bf16[64,8,8,128]{3,2,1,0:T(8,128)(2,1)}, u32[]{:S(2)}) copy-start(bf16[64,8,8,128]{3,2,1,0:T(8,128)(2,1)} %fusion.12) | copy-start | bytes 3145732
Sparse Core Ops, SparseCore 0:
  12.0 128.2 all-gather.11
  144.7 125.8 all-gather.9
  275.1 126.2 all-gather.13
  403.4 52.3 all-gather.7
  1149.5 903.1 reduce-scatter.2
where the time goes:
time: 2060 us
  blocking collectives  1400 us (68%)
  waiting for transfers between devices  597 us (29%)
  local copies, waits for them, and re-layouts  24.8 us (1%)
    unnamed x1, blocking collectives  727 us
    pmax x1, blocking collectives, largest_scores(): return lax.pmax(jnp.max(masked, axis=2), 'frame')  668 us
    reduce_scatter x1, waiting for transfers between devices, shards(): lax.psum_scatter(numer, 'frame', scatter_dimension=1, tiled=True)  168 us
    all_gather x1, waiting for transfers between devices, shards(): lax.all_gather(w_value, 'frame', axis=0, tiled=True)  127 us
    all_gather x1, waiting for transfers between devices, shards(): lax.all_gather(w_key, 'frame', axis=0, tiled=True)  126 us
    all_gather x1, waiting for transfers between devices, shards(): every_query = lax.all_gather(queries, 'frame', axis=0, tiled=True)  125 us
    all_gather x1, waiting for transfers between devices, shards(): every = lax.all_gather(blocks_held, 'head', axis=0, tiled=True)  48.8 us
  transfers between devices with their start and end apart: 5, of which 5 were waited for; matrix products, arithmetic and copies ran while one was open for 1% of the time, Pallas kernels for 0%

commit v1 on v0

v1 whole, which is shorter than its diff:
```python
import functools
import math

import jax
import jax.numpy as jnp
from jax import lax
from jax.experimental import pallas as pl
from jax.experimental.pallas import tpu as pltpu
from jax.sharding import Mesh, PartitionSpec as P

HEAD_DIM = 128
LAT_BLK = 2
BLK = 128
NB = 4
MEDIA = 1152
LAT = 768
NUM_LAT = 256
VIDEOS = 3
NX, NY, NZ = 4, 4, 8
PAIR = 2
HEADS_HERE = 4
COLS = HEADS_HERE * HEAD_DIM
WIDE = COLS + 128
ROWS = PAIR * NB * BLK
OWN = 6
SCALE2 = HEAD_DIM ** (-0.5) * math.log2(math.e)
EMPTY = -1e30
VMEM = pl.BlockSpec(memory_space=pltpu.VMEM)
SMEM = pl.BlockSpec(memory_space=pltpu.SMEM)


def norm_kernel(slot_ref, rows_ref, gain_ref, out_ref):
    values = rows_ref[0].astype(jnp.float32)
    center = values - jnp.mean(values, axis=1, keepdims=True)
    spread = jnp.mean(center * center, axis=1, keepdims=True)
    out_ref[0] = (center * lax.rsqrt(spread + 1e-6) * gain_ref[...]).astype(jnp.bfloat16)


def norm_slots(slots, blocks, media_gain):
    return pl.pallas_call(
        norm_kernel,
        grid_spec=pltpu.PrefetchScalarGridSpec(
            num_scalar_prefetch=1,
            grid=(2,),
            in_specs=[
                pl.BlockSpec((1, BLK, MEDIA), lambda i, s: (s[i], 0, 0)),
                pl.BlockSpec((1, MEDIA), lambda i, s: (0, 0)),
            ],
            out_specs=pl.BlockSpec((1, BLK, MEDIA), lambda i, s: (i, 0, 0)),
        ),
        out_shape=jax.ShapeDtypeStruct((2, BLK, MEDIA), jnp.bfloat16),
        name="norm_slots",
    )(slots, blocks, media_gain.reshape(1, MEDIA))


def split_words(value):
    high = value.astype(jnp.bfloat16).astype(jnp.float32)
    return high, value - high


def lay_words(lane, head, top, total, extras):
    for k, word in enumerate((*split_words(top), *split_words(total))):
        extras = jnp.where(lane == 4 * head + k, word, extras)
    return extras


def attend_kernel(info_ref, mine_ref, other_ref, wk_ref, wv_ref, q_ref, place_row_ref, place_col_ref, out_ref, rows, acc, sem):
    def copy(b, src):
        return pltpu.make_async_copy(
            src.at[info_ref[8 + b]], rows.at[pl.ds(b * BLK, BLK)], sem.at[b]
        )

    for b in range(PAIR * NB):
        @pl.when(info_ref[b] == 0)
        def _():
            copy(b, mine_ref).start()

        @pl.when(info_ref[b] != 0)
        def _():
            copy(b, other_ref).start()
    acc[...] = jnp.zeros_like(acc)
    for b in range(PAIR * NB):
        copy(b, mine_ref).wait()
    x = rows[...]
    keys = jnp.dot(x, wk_ref[...], preferred_element_type=jnp.float32).astype(jnp.bfloat16)
    values = jnp.dot(x, wv_ref[...], preferred_element_type=jnp.float32).astype(jnp.bfloat16)
    base = info_ref[16]
    ends = (info_ref[17], info_ref[18], info_ref[19])
    position = base + lax.broadcasted_iota(jnp.int32, (1, ROWS), 1)
    for v in range(VIDEOS):
        first = 0 if v == 0 else ends[v - 1]
        last = ends[v]

        @pl.when((first < base + ROWS) & (last > base) & (first < last))
        def _():
            allowed = (position >= first) & (position < last)
            pick = (
                place_row_ref[...] == v * NUM_LAT + lax.broadcasted_iota(jnp.int32, (NUM_LAT, LAT), 0)
            ).astype(jnp.bfloat16)
            put = (
                place_col_ref[...] == v * NUM_LAT + lax.broadcasted_iota(jnp.int32, (LAT, NUM_LAT), 1)
            ).astype(jnp.bfloat16)
            queries = jnp.dot(pick, q_ref[...], preferred_element_type=jnp.float32).astype(jnp.bfloat16)
            lane = lax.broadcasted_iota(jnp.int32, (NUM_LAT, 128), 1)
            extras = jnp.zeros((NUM_LAT, 128), jnp.float32)
            for h in range(HEADS_HERE):
                cols = slice(h * HEAD_DIM, (h + 1) * HEAD_DIM)
                scores = lax.dot_general(
                    queries[:, cols],
                    keys[:, cols],
                    (((1,), (1,)), ((), ())),
                    preferred_element_type=jnp.float32,
                ) * SCALE2
                scores = jnp.where(allowed, scores, EMPTY)
                high, low = split_words(jnp.max(scores, axis=1, keepdims=True))
                top = high + low.astype(jnp.bfloat16).astype(jnp.float32)
                weights = jnp.where(allowed, jnp.exp2(scores - top), 0.0)
                total = jnp.sum(weights, axis=1, keepdims=True)
                numer = jnp.dot(
                    weights.astype(jnp.bfloat16), values[:, cols], preferred_element_type=jnp.float32
                )
                extras = lay_words(lane, h, top, total, extras)
                acc[:, cols] += jnp.dot(put, numer.astype(jnp.bfloat16), preferred_element_type=jnp.float32)
            acc[:, COLS:] += jnp.dot(put, extras.astype(jnp.bfloat16), preferred_element_type=jnp.float32)

    out_ref[...] = acc[...].astype(jnp.bfloat16)


def attend(info, mine, other, wk, wv, q, place):
    return pl.pallas_call(
        attend_kernel,
        in_specs=[SMEM, pl.BlockSpec(memory_space=pl.ANY), pl.BlockSpec(memory_space=pl.ANY)] + [VMEM] * 5,
        out_specs=VMEM,
        out_shape=jax.ShapeDtypeStruct((LAT, WIDE), jnp.bfloat16),
        scratch_shapes=[
            pltpu.VMEM((ROWS, MEDIA), jnp.bfloat16),
            pltpu.VMEM((LAT, WIDE), jnp.float32),
            pltpu.SemaphoreType.DMA((PAIR * NB,)),
        ],
        compiler_params=pltpu.CompilerParams(vmem_limit_bytes=48 * 1024 * 1024),
        name="attend",
    )(info, mine, other, wk, wv, q, place.reshape(1, LAT), place.reshape(LAT, 1))


def gather_words(extras, head):
    top = extras[..., 4 * head:4 * head + 1] + extras[..., 4 * head + 1:4 * head + 2]
    total = extras[..., 4 * head + 2:4 * head + 3] + extras[..., 4 * head + 3:4 * head + 4]
    return jnp.where(total > 0, top, EMPTY), total


def merge_kernel(parts_ref, out_ref):
    rows = LAT // NX
    lane = lax.broadcasted_iota(jnp.int32, (rows, 128), 1)
    extras_in = parts_ref[:, :, COLS:].astype(jnp.float32)
    extras = jnp.zeros((rows, 128), jnp.float32)
    spread_rows = NY * NZ * 8
    target = lax.broadcasted_iota(jnp.int32, (spread_rows, rows), 0)
    source = lax.broadcasted_iota(jnp.int32, (spread_rows, rows), 1)
    put = ((target // 8 * OWN + target % 8 == source) & (target % 8 < OWN)).astype(jnp.bfloat16)
    for h in range(HEADS_HERE):
        cols = slice(h * HEAD_DIM, (h + 1) * HEAD_DIM)
        top, total = gather_words(extras_in, h)
        best = jnp.max(top, axis=0)
        factor = jnp.where(total > 0, jnp.exp2(top - best[None]), 0.0)
        whole = jnp.sum(total * factor, axis=0)
        numer = jnp.sum(parts_ref[:, :, cols].astype(jnp.float32) * factor, axis=0)
        extras = lay_words(lane, h, jnp.where(whole > 0, best, 0.0), whole, extras)
        moved = jnp.dot(put, numer.astype(jnp.bfloat16), preferred_element_type=jnp.float32)
        out_ref[:, :, cols] = moved.astype(jnp.bfloat16).reshape(NY * NZ, 8, HEAD_DIM)
    moved = jnp.dot(put, extras.astype(jnp.bfloat16), preferred_element_type=jnp.float32)
    out_ref[:, :, COLS:] = moved.astype(jnp.bfloat16).reshape(NY * NZ, 8, 128)


def merge(parts):
    return pl.pallas_call(
        merge_kernel,
        in_specs=[VMEM],
        out_specs=VMEM,
        out_shape=jax.ShapeDtypeStruct((NY * NZ, 8, WIDE), jnp.bfloat16),
        name="merge",
    )(parts)


def finish_kernel(parts_ref, out_ref):
    groups = NY * NZ // PAIR
    for part in range(PAIR):
        extras = parts_ref[:, part, :, COLS:].astype(jnp.float32)
        for h in range(HEADS_HERE):
            cols = slice(h * HEAD_DIM, (h + 1) * HEAD_DIM)
            top, total = gather_words(extras, h)
            best = jnp.max(top, axis=0)
            factor = jnp.where(total > 0, jnp.exp2(top - best[None]), 0.0)
            whole = jnp.sum(total * factor, axis=0)
            numer = jnp.sum(parts_ref[:, part, :, cols].astype(jnp.float32) * factor, axis=0)
            result = (numer / whole).astype(jnp.bfloat16)
            start = part * COLS + h * HEAD_DIM
            out_ref[:, start:start + HEAD_DIM] = result[:OWN]


def finish(parts):
    return pl.pallas_call(
        finish_kernel,
        in_specs=[VMEM],
        out_specs=VMEM,
        out_shape=jax.ShapeDtypeStruct((OWN, PAIR * COLS), jnp.bfloat16),
        name="finish",
    )(parts.reshape(NY * NZ // PAIR, PAIR, 8, WIDE))


def exchange(value, axis):
    return lax.all_to_all(value, axis, split_axis=0, concat_axis=0, tiled=True)


def spread(value, axis, count):
    return exchange(jnp.broadcast_to(value[None], (count,) + value.shape), axis)


def shards(
    encoded,
    block_source,
    block_slot,
    video_patches,
    latent_video,
    media_gain,
    queries,
    w_key,
    w_value,
):
    ax, ay, az = lax.axis_index("x"), lax.axis_index("yh"), lax.axis_index("z")
    al, ac = lax.axis_index("yl"), lax.axis_index("c")
    head = al * 2 + ac
    swap_z = [(i, i ^ 1) for i in range(NZ)]
    swap = [(0, 1), (1, 0)]

    slot = lax.dynamic_index_in_dim(block_slot[0], head, 0, keepdims=False)[:2]
    own = norm_slots(slot, encoded.reshape(NB, BLK, MEDIA), media_gain)
    near_y = lax.ppermute(own, "yl", swap)
    near_z = lax.ppermute(own, "z", swap_z)
    source_z = lax.ppermute(block_source, "z", swap_z)

    local = jnp.concatenate([w_key, w_value, queries], axis=0)
    rows = local.shape[0]
    local = jnp.transpose(local.reshape(rows, PAIR, COLS), (1, 0, 2))
    line = exchange(jnp.tile(local, (NZ // PAIR, 1, 1)), "z")
    line = jnp.concatenate(
        [line[:, :9].reshape(72, COLS), line[:, 9:18].reshape(72, COLS), line[:, 18:].reshape(48, COLS)], axis=0
    )
    far_y = lax.ppermute(near_z[0:1], "yl", swap)
    far_z = lax.ppermute(near_y[1:2], "z", swap_z)
    plane = spread(line, "yh", NY)
    plane_k = plane[:, :72].reshape(288, COLS)
    plane_v = plane[:, 72:144].reshape(288, COLS)
    plane_q = plane[:, 144:].reshape(192, COLS)
    mine = jnp.concatenate([own, near_y, near_z, far_y, far_z], axis=0)
    other = lax.ppermute(mine, "c", swap)
    cube = spread(jnp.concatenate([plane_k, plane_q, plane_v], axis=0), "x", NX)
    wk = cube[:, :288].reshape(MEDIA, COLS)
    q = cube[:, 288:480].reshape(LAT, COLS)
    wv = cube[:, 480:].reshape(MEDIA, COLS)

    part = az % PAIR
    pair_source = jnp.where(
        part == 0,
        jnp.concatenate([block_source[:, 0], source_z[:, 0]]),
        jnp.concatenate([source_z[:, 0], block_source[:, 0]]),
    )
    block = jnp.arange(PAIR * NB, dtype=jnp.int32)
    same = (pair_source[:, None] == pair_source[None, :]) & (block[None, :] < block[:, None])
    same = same & (block[:, None] // NB == block[None, :] // NB)
    rank = jnp.sum(same.astype(jnp.int32), axis=1)
    place_in = ((block // NB) ^ part) * 4 + ((pair_source // 2) ^ al) * 2 + rank
    ends = jnp.cumsum(video_patches)
    base = (ax * (NY * NZ) + ay * NZ + az - part) * (NB * BLK)
    info = jnp.concatenate(
        [(pair_source % 2) ^ ac, place_in, base[None].astype(jnp.int32), ends.astype(jnp.int32)]
    ).astype(jnp.int32)

    which = (latent_video[:, None] == jnp.arange(VIDEOS)[None, :]).astype(jnp.int32)
    before = jnp.cumsum(which, axis=0) - which
    block_place = latent_video * NUM_LAT + LAT_BLK * jnp.sum(before * which, axis=1)
    place = (block_place[:, None] + jnp.arange(LAT_BLK)[None, :]).reshape(-1).astype(jnp.int32)

    message = attend(info, mine, other, wk, wv, q, place)
    merged = merge(exchange(message.reshape(NX, LAT // NX, WIDE), "x"))
    return finish(exchange(merged, ("yh", "z")))


def solution(mesh):
    grid = Mesh(mesh.devices.reshape(NX, NY, NZ, 2, 2), ("x", "yh", "z", "yl", "c"))
    frame, head = ("x", "yh", "z"), ("yl", "c")
    placed = (
        P(frame + head, None),
        P(frame, None),
        P(frame, None, None),
        P(),
        P(),
        P(),
        P(frame, head),
        P(frame, head),
        P(frame, head),
    )
    return jax.shard_map(
        shards, mesh=grid, in_specs=placed, out_specs=P(frame, head), check_vma=False
    )
```

time: 2060 us -> 158 us (0.08)
  the two profiles are of different devices: /device:TPU:2 before, /device:TPU:16 now
where the time goes in v1:
time: 158 us; the launch traced here: 157 us
  waiting for transfers between devices  48 us (30%)
  starting transfers between devices  37.5 us (24%)
  blocking collectives  35.2 us (22%)
  Pallas kernels  17.2 us (11%)
  local copies, waits for them, and re-layouts  14.9 us (9%)
  other arithmetic  4.16 us (3%)
    all_to_all x2, blocking collectives, exchange(): return lax.all_to_all(value, axis, split_axis=0, concat_axis=0, tiled=True)  35.2 us
    all_to_all x3, waiting for transfers between devices, exchange(): return lax.all_to_all(value, axis, split_axis=0, concat_axis=0, tiled=True)  32.1 us
    all_to_all x3, starting transfers between devices, exchange(): return lax.all_to_all(value, axis, split_axis=0, concat_axis=0, tiled=True)  22.2 us
    pallas_call x1, Pallas kernels, attend(): pl.pallas_call(attend_kernel, in_specs=[SMEM, pl.BlockSpec(memory_space=p...  9.05 us
    ppermute x1, waiting for transfers between devices, shards(): near_y = lax.ppermute(own, 'yl', swap)  8.22 us
    ppermute x1, waiting for transfers between devices, shards(): near_z = lax.ppermute(own, 'z', swap_z)  7.64 us
    unnamed x14, local copies, waits for them, and re-layouts  5.12 us
    ppermute x1, starting transfers between devices, shards(): source_z = lax.ppermute(block_source, 'z', swap_z)  3.92 us
  transfers between devices with their start and end apart: 9, of which 4 were waited for; matrix products, arithmetic and copies ran while one was open for 10% of the time, Pallas kernels for 2%

profile of v1, /device:TPU:16, one launch (start us, length us, event | category | flops | bytes accessed | tf_op | source)
XLA Modules:
  0.0 157.3 jit_solution(18350707153210380948)
XLA Ops:
  0.0 0.0 copy-start
  0.0 0.8 pad_maximum_fusion.2
  0.9 0.0 copy-start.3
  0.9 0.7 tile.4
  1.6 10.3 %all-to-all-start = ((bf16[8,24,512]{2,1,0:T(8,128)(2,1)}), bf16[8,24,512]{2,1,0:T(8,128)(2,1)S(1)}, u32[]{:S(2)}, u32[]{:S(2)}) async-start(bf16[8,24,512]{2,1,0:T(8,128)(2,1)} %bitcast.8), calls=%async_computation | async-start | bytes 393216 | tf_op jit(solution)/shard_map/all_to_all | solution.py:211
  11.9 0.0 copy-done
  11.9 10.5 %all-to-all-done = bf16[8,24,512]{2,1,0:T(8,128)(2,1)S(1)} async-done(((bf16[8,24,512]{2,1,0:T(8,128)(2,1)}), bf16[8,24,512]{2,1,0:T(8,128)(2,1)S(1)}, u32[]{:S(2)}, u32[]{:S(2)}) %all-to-all-start) | async-done | bytes 196640 | tf_op jit(solution)/shard_map/all_to_all | solution.py:211
  22.6 1.0 broadcast_in_dim.7
  23.5 7.4 %all-to-all-start.1 = ((bf16[4,192,512]{2,1,0:T(8,128)(2,1)}), bf16[4,192,512]{2,1,0:T(8,128)(2,1)S(1)}, u32[]{:S(2)}, u32[]{:S(2)}) async-start(bf16[4,192,512]{2,1,0:T(8,128)(2,1)} %broadcast_in_dim.7), calls=%async_computation.1 | async-start | bytes 1572864 | tf_op jit(solution)/shard_map/all_to_all | solution.py:211
  31.0 0.5 slice_bitcast_fusion.slot_ref
  31.5 0.0 copy-done.3
  31.5 0.6 reshape.277.gain_ref
  32.1 2.9 %norm_slots.1 = bf16[2,128,1152]{2,1,0:T(8,128)(2,1)} custom-call(s32[2]{0:T(128)} %slice_bitcast_fusion.slot_ref, bf16[4,128,1152]{2,1,0:T(8,128)(2,1)} %bitcast.43, f32[1,1152]{1,0:T(1,128)} %reshape.277.gain_ref), custom_call_target="tpu_custom_call" | custom-call | tf_op jit(solution)/shard_map/norm_slots/pallas_call | solution.py:40
  35.0 2.5 %collective-permute-start.2 = (bf16[2,128,1152]{2,1,0:T(8,128)(2,1)}, bf16[2,128,1152]{2,1,0:T(8,128)(2,1)S(1)}, u32[]{:S(2)}, u32[]{:S(2)}) collective-permute-start(bf16[2,128,1152]{2,1,0:T(8,128)(2,1)} %norm_slots.1), channel_id=1, source_target_pairs={{0,4},{4,0},{8,12},{12,8},{16,20},{20,16},{24,28},{28,24},{1,5},{5... | collective-permute-start | bytes 1769480 | tf_op jit(solution)/shard_map/ppermute | solution.py:238
  37.5 2.6 %collective-permute-start.1 = (bf16[2,128,1152]{2,1,0:T(8,128)(2,1)}, bf16[2,128,1152]{2,1,0:T(8,128)(2,1)S(1)}, u32[]{:S(2)}, u32[]{:S(2)}) collective-permute-start(bf16[2,128,1152]{2,1,0:T(8,128)(2,1)} %norm_slots.1), channel_id=1, source_target_pairs={{0,2},{2,0},{1,3},{3,1},{4,6},{6,4},{5,7},{7,5},{8,10},{10,8},{9,1... | collective-permute-start | bytes 1769480 | tf_op jit(solution)/shard_map/ppermute | solution.py:237
  40.1 2.0 %constant_dynamic-update-slice_fusion.4 = bf16[8,128,1152]{2,1,0:T(8,128)(2,1)} fusion(bf16[2,128,1152]{2,1,0:T(8,128)(2,1)} %norm_slots.1), kind=kLoop, calls=%fused_computation.8 | loop fusion | bytes 1179648
  42.0 7.6 %collective-permute-done.2 = bf16[2,128,1152]{2,1,0:T(8,128)(2,1)S(1)} collective-permute-done((bf16[2,128,1152]{2,1,0:T(8,128)(2,1)}, bf16[2,128,1152]{2,1,0:T(8,128)(2,1)S(1)}, u32[]{:S(2)}, u32[]{:S(2)}) %collective-permute-start.2) | collective-permute-done | bytes 589856 | tf_op jit(solution)/shard_map/ppermute | solution.py:238
  49.7 0.7 slice.60
  50.4 2.6 %collective-permute-start.3 = (bf16[1,128,1152]{2,1,0:T(8,128)(2,1)}, bf16[1,128,1152]{2,1,0:T(8,128)(2,1)S(1)}, u32[]{:S(2)}, u32[]{:S(2)}) collective-permute-start(bf16[1,128,1152]{2,1,0:T(8,128)(2,1)} %slice.60), channel_id=1, source_target_pairs={{0,2},{2,0},{1,3},{3,1},{4,6},{6,4},{5,7},{7,5},{8,10},{10,8},{9,1... | collective-permute-start | bytes 884744 | tf_op jit(solution)/shard_map/ppermute | solution.py:248
  53.0 8.2 %collective-permute-done.1 = bf16[2,128,1152]{2,1,0:T(8,128)(2,1)S(1)} collective-permute-done((bf16[2,128,1152]{2,1,0:T(8,128)(2,1)}, bf16[2,128,1152]{2,1,0:T(8,128)(2,1)S(1)}, u32[]{:S(2)}, u32[]{:S(2)}) %collective-permute-start.1) | collective-permute-done | bytes 589856 | tf_op jit(solution)/shard_map/ppermute | solution.py:237
  61.2 0.7 slice.61
  61.9 1.9 %collective-permute-start.4 = (bf16[1,128,1152]{2,1,0:T(8,128)(2,1)}, bf16[1,128,1152]{2,1,0:T(8,128)(2,1)}, u32[]{:S(2)}, u32[]{:S(2)}) collective-permute-start(bf16[1,128,1152]{2,1,0:T(8,128)(2,1)} %slice.61), channel_id=1, source_target_pairs={{0,4},{4,0},{8,12},{12,8},{16,20},{20,16},{24,28},{28,24},{1,5},{5... | collective-permute-start | bytes 884744 | tf_op jit(solution)/shard_map/ppermute | solution.py:249
  63.9 0.9 constant_dynamic-update-slice_fusion.3
  64.7 0.9 constant_dynamic-update-slice_fusion.2
  65.6 0.0 all-to-all-done.1
  65.7 0.1 pad_maximum_fusion
  65.7 1.9 %broadcast_in_dim.8 = bf16[4,768,512]{2,1,0:T(8,128)(2,1)} broadcast(bf16[768,512]{1,0:T(8,128)(2,1)S(1)} %pad_maximum_fusion), dimensions={1,2} | broadcast | bytes 3932160 | tf_op jit(solution)/shard_map/broadcast_in_dim | solution.py:215
  67.6 0.0 copy-start.4
  67.6 0.0 copy-start.2
  67.6 4.4 %all-to-all-start.2 = ((bf16[4,768,512]{2,1,0:T(8,128)(2,1)}), bf16[4,768,512]{2,1,0:T(8,128)(2,1)S(1)}, u32[]{:S(2)}, u32[]{:S(2)}) async-start(bf16[4,768,512]{2,1,0:T(8,128)(2,1)} %broadcast_in_dim.8), calls=%async_computation.2 | async-start | bytes 6291456 | tf_op jit(solution)/shard_map/all_to_all | solution.py:211
  72.1 0.0 collective-permute-done.3
  72.1 0.7 constant_dynamic-update-slice_fusion.1
  72.8 0.0 collective-permute-done.4
  72.8 1.7 %constant_dynamic-update-slice_fusion.mine_ref = bf16[8,128,1152]{2,1,0:T(8,128)(2,1)} fusion(bf16[8,128,1152]{2,1,0:T(8,128)(2,1)} %constant_dynamic-update-slice_fusion.1, bf16[1,128,1152]{2,1,0:T(8,128)(2,1)} %collective-permute-done.4), kind=kLoop, calls=%fused_computation.4 | loop fusion | bytes 589824 | tf_op jit(solution)/shard_map/concatenate | solution.py:254
  74.5 1.9 %collective-permute-start.5 = (bf16[8,128,1152]{2,1,0:T(8,128)(2,1)}, bf16[8,128,1152]{2,1,0:T(8,128)(2,1)}, u32[]{:S(2)}, u32[]{:S(2)}) collective-permute-start(bf16[8,128,1152]{2,1,0:T(8,128)(2,1)} %constant_dynamic-update-slice_fusion.mine_ref), channel_id=1, source_target_pairs={{0,1},{1,0},{2,3},{3,2},{4,5},{5,4},{6,7},{7,6},{8,9},{9,8},{10,11... | collective-permute-start | bytes 7077896 | tf_op jit(solution)/shard_map/ppermute | solution.py:255
  76.4 0.0 copy-done.4
  76.4 3.9 %collective-permute-start = (s32[4,1]{0,1:T(1,128)S(1)}, s32[4,1]{0,1:T(1,128)}, u32[]{:S(2)}, u32[]{:S(2)}) collective-permute-start(s32[4,1]{0,1:T(1,128)S(1)} %copy-done.4), channel_id=1, source_target_pairs={{0,4},{4,0},{8,12},{12,8},{16,20},{20,16},{24,28},{28,24},{1,5},{5... | collective-permute-start | bytes 56 | tf_op jit(solution)/shard_map/ppermute | solution.py:239
  80.4 0.0 copy-done.2
  80.4 0.9 reduce-window.20
  81.3 0.2 slice_reduce_fusion
  81.5 0.2 reduce-window.21
  81.7 0.1 add_bitcast_fusion
  81.8 0.1 iota_add_fusion
  81.9 0.0 copy-start.1
  82.0 0.7 copy-done.1
  82.6 0.2 add.91.place_row_ref
  82.8 1.1 add.93.place_col_ref
  83.9 0.8 reduce-window.19
  84.7 0.0 collective-permute-done
  84.7 0.8 fusion.6
  85.5 0.2 convert_reduce_fusion
  85.7 0.1 pad_add_fusion.info_ref
  85.8 21.6 %all-to-all-done.2 = bf16[4,768,512]{2,1,0:T(8,128)(2,1)S(1)} async-done(((bf16[4,768,512]{2,1,0:T(8,128)(2,1)}), bf16[4,768,512]{2,1,0:T(8,128)(2,1)S(1)}, u32[]{:S(2)}, u32[]{:S(2)}) %all-to-all-start.2) | async-done | bytes 3145760 | tf_op jit(solution)/shard_map/all_to_all | solution.py:211
  107.4 0.1 slice.70
  107.5 0.3 fusion.7
  107.8 0.0 collective-permute-done.5.other_ref
  107.8 9.0 %attend.1 = bf16[768,640]{1,0:T(8,128)(2,1)S(1)} custom-call(s32[20]{0:T(128)S(1)} %pad_add_fusion.info_ref, bf16[8,128,1152]{2,1,0:T(8,128)(2,1)} %constant_dynamic-update-slice_fusion.mine_ref, bf16[8,128,1152]{2,1,0:T(8,128)(2,1)} %collective-permute-done.5.other_ref, bf16[1152,512]{1,0:T(8,128)(2,1)S(1)} %bitcast.39, bf16[1152,512]{1,0:T(8,128)(2,1)S(1)} %bitcast.38, ...), custom_call_target="tpu_custom_call" | custom-call | tf_op jit(solution)/shard_map/attend/pallas_call | solution.py:130
  116.8 14.4 %all_to_all.25.parts_ref = bf16[4,192,640]{2,1,0:T(8,128)(2,1)} all-to-all(bf16[4,192,640]{2,1,0:T(8,128)(2,1)S(1)} %bitcast.40), channel_id=1, replica_groups=mesh['x'=4,'yh'=4,'z'=8,'yl'=2,'c'=2] {'x'}, dimensions={0} | all-to-all | bytes 1966080 | tf_op jit(solution)/shard_map/all_to_all | solution.py:211
  131.2 3.3 %merge.1 = bf16[32,8,640]{2,1,0:T(8,128)(2,1)} custom-call(bf16[4,192,640]{2,1,0:T(8,128)(2,1)} %all_to_all.25.parts_ref), custom_call_target="tpu_custom_call" | custom-call | tf_op jit(solution)/shard_map/merge/pallas_call | solution.py:175
  134.5 20.8 %all_to_all.26 = bf16[32,8,640]{2,1,0:T(8,128)(2,1)} all-to-all(bf16[32,8,640]{2,1,0:T(8,128)(2,1)} %merge.1), channel_id=1, replica_groups=mesh['x'=4,'yh'=4,'z'=8,'yl'=2,'c'=2] {'yh','z'}, dimensions={0} | all-to-all | bytes 655360 | tf_op jit(solution)/shard_map/all_to_all | solution.py:211
  155.3 2.0 %finish.1 = bf16[6,1024]{1,0:T(8,128)(2,1)} custom-call(bf16[16,2,8,640]{3,2,1,0:T(8,128)(2,1)} %bitcast.42), custom_call_target="tpu_custom_call" | custom-call | tf_op jit(solution)/shard_map/finish/pallas_call | solution.py:201
  (16 shorter events, 0.3 us)
Async XLA Ops:
  0.0 11.9 %copy-start = (s32[1,4,4]{2,1,0:T(4,128)S(1)}, s32[1,4,4]{2,1,0:T(4,128)}, u32[]{:S(2)}) copy-start(s32[1,4,4]{2,1,0:T(4,128)} %param.11) | copy-start | bytes 196
  0.9 30.6 %copy-start.3 = (f32[1152]{0:T(1024)S(1)}, f32[1152]{0:T(1024)}, u32[]{:S(2)}) copy-start(f32[1152]{0:T(1024)} %param.14) | copy-start | bytes 13828
  1.6 20.8 %all-to-all-start = ((bf16[8,24,512]{2,1,0:T(8,128)(2,1)}), bf16[8,24,512]{2,1,0:T(8,128)(2,1)S(1)}, u32[]{:S(2)}, u32[]{:S(2)}) async-start(bf16[8,24,512]{2,1,0:T(8,128)(2,1)} %bitcast.8), calls=%async_computation | async-start | bytes 393216 | tf_op jit(solution)/shard_map/all_to_all | solution.py:211
  23.5 42.1 %all-to-all-start.1 = ((bf16[4,192,512]{2,1,0:T(8,128)(2,1)}), bf16[4,192,512]{2,1,0:T(8,128)(2,1)S(1)}, u32[]{:S(2)}, u32[]{:S(2)}) async-start(bf16[4,192,512]{2,1,0:T(8,128)(2,1)} %broadcast_in_dim.7), calls=%async_computation.1 | async-start | bytes 1572864 | tf_op jit(solution)/shard_map/all_to_all | solution.py:211
  35.0 14.7 %collective-permute-start.2 = (bf16[2,128,1152]{2,1,0:T(8,128)(2,1)}, bf16[2,128,1152]{2,1,0:T(8,128)(2,1)S(1)}, u32[]{:S(2)}, u32[]{:S(2)}) collective-permute-start(bf16[2,128,1152]{2,1,0:T(8,128)(2,1)} %norm_slots.1), channel_id=1, source_target_pairs={{0,4},{4,0},{8,12},{12,8},{16,20},{20,16},{24,28},{28,24},{1,5},{5... | collective-permute-start | bytes 1769480 | tf_op jit(solution)/shard_map/ppermute | solution.py:238
  37.5 23.7 %collective-permute-start.1 = (bf16[2,128,1152]{2,1,0:T(8,128)(2,1)}, bf16[2,128,1152]{2,1,0:T(8,128)(2,1)S(1)}, u32[]{:S(2)}, u32[]{:S(2)}) collective-permute-start(bf16[2,128,1152]{2,1,0:T(8,128)(2,1)} %norm_slots.1), channel_id=1, source_target_pairs={{0,2},{2,0},{1,3},{3,1},{4,6},{6,4},{5,7},{7,5},{8,10},{10,8},{9,1... | collective-permute-start | bytes 1769480 | tf_op jit(solution)/shard_map/ppermute | solution.py:237
  50.4 21.7 %collective-permute-start.3 = (bf16[1,128,1152]{2,1,0:T(8,128)(2,1)}, bf16[1,128,1152]{2,1,0:T(8,128)(2,1)S(1)}, u32[]{:S(2)}, u32[]{:S(2)}) collective-permute-start(bf16[1,128,1152]{2,1,0:T(8,128)(2,1)} %slice.60), channel_id=1, source_target_pairs={{0,2},{2,0},{1,3},{3,1},{4,6},{6,4},{5,7},{7,5},{8,10},{10,8},{9,1... | collective-permute-start | bytes 884744 | tf_op jit(solution)/shard_map/ppermute | solution.py:248
  61.9 10.9 %collective-permute-start.4 = (bf16[1,128,1152]{2,1,0:T(8,128)(2,1)}, bf16[1,128,1152]{2,1,0:T(8,128)(2,1)}, u32[]{:S(2)}, u32[]{:S(2)}) collective-permute-start(bf16[1,128,1152]{2,1,0:T(8,128)(2,1)} %slice.61), channel_id=1, source_target_pairs={{0,4},{4,0},{8,12},{12,8},{16,20},{20,16},{24,28},{28,24},{1,5},{5... | collective-permute-start | bytes 884744 | tf_op jit(solution)/shard_map/ppermute | solution.py:249
  67.6 8.8 %copy-start.4 = (s32[4,1]{0,1:T(1,128)S(1)}, s32[4,1]{0,1:T(1,128)}, u32[]{:S(2)}) copy-start(s32[4,1]{0,1:T(1,128)} %param.10) | copy-start | bytes 52
  67.6 12.7 %copy-start.2 = (s32[384]{0:T(512)S(1)}, s32[384]{0:T(512)}, u32[]{:S(2)}) copy-start(s32[384]{0:T(512)} %param.13) | copy-start | bytes 4612
  67.6 39.8 %all-to-all-start.2 = ((bf16[4,768,512]{2,1,0:T(8,128)(2,1)}), bf16[4,768,512]{2,1,0:T(8,128)(2,1)S(1)}, u32[]{:S(2)}, u32[]{:S(2)}) async-start(bf16[4,768,512]{2,1,0:T(8,128)(2,1)} %broadcast_in_dim.8), calls=%async_computation.2 | async-start | bytes 6291456 | tf_op jit(solution)/shard_map/all_to_all | solution.py:211
  74.5 33.3 %collective-permute-start.5 = (bf16[8,128,1152]{2,1,0:T(8,128)(2,1)}, bf16[8,128,1152]{2,1,0:T(8,128)(2,1)}, u32[]{:S(2)}, u32[]{:S(2)}) collective-permute-start(bf16[8,128,1152]{2,1,0:T(8,128)(2,1)} %constant_dynamic-update-slice_fusion.mine_ref), channel_id=1, source_target_pairs={{0,1},{1,0},{2,3},{3,2},{4,5},{5,4},{6,7},{7,6},{8,9},{9,8},{10,11... | collective-permute-start | bytes 7077896 | tf_op jit(solution)/shard_map/ppermute | solution.py:255
  76.4 8.3 %collective-permute-start = (s32[4,1]{0,1:T(1,128)S(1)}, s32[4,1]{0,1:T(1,128)}, u32[]{:S(2)}, u32[]{:S(2)}) collective-permute-start(s32[4,1]{0,1:T(1,128)S(1)} %copy-done.4), channel_id=1, source_target_pairs={{0,4},{4,0},{8,12},{12,8},{16,20},{20,16},{24,28},{28,24},{1,5},{5... | collective-permute-start | bytes 56 | tf_op jit(solution)/shard_map/ppermute | solution.py:239
  81.9 0.7 copy-start.1

commit v2 on v1

v2 whole, which is shorter than its diff:
```python
import functools
import math

import jax
import jax.numpy as jnp
from jax import lax
from jax.experimental import pallas as pl
from jax.experimental.pallas import tpu as pltpu
from jax.sharding import Mesh, PartitionSpec as P

HEAD_DIM = 128
LAT_BLK = 2
BLK = 128
NB = 4
MEDIA = 1152
LAT = 768
NUM_LAT = 256
VIDEOS = 3
NX, NY, NZ = 4, 4, 8
PARTS = 4
HEADS_HERE = 2
COLS = HEADS_HERE * HEAD_DIM
PADDED = 128 * 8
FRAME_ROWS = NB * BLK
ROWS = PARTS * FRAME_ROWS
BLOCKS = PARTS * NB
RING = 8
OWN = 6
SCALE2 = HEAD_DIM ** (-0.5) * math.log2(math.e)
EMPTY = -1e30
VMEM = pl.BlockSpec(memory_space=pltpu.VMEM)
SMEM = pl.BlockSpec(memory_space=pltpu.SMEM)


def norm_kernel(slot_ref, rows_ref, gain_ref, out_ref):
    values = rows_ref[0].astype(jnp.float32)
    center = values - jnp.mean(values, axis=1, keepdims=True)
    spread = jnp.mean(center * center, axis=1, keepdims=True)
    out_ref[0] = (center * lax.rsqrt(spread + 1e-6) * gain_ref[...][None, :]).astype(jnp.bfloat16)


def norm_slots(slots, blocks, media_gain):
    return pl.pallas_call(
        norm_kernel,
        grid_spec=pltpu.PrefetchScalarGridSpec(
            num_scalar_prefetch=1,
            grid=(2,),
            in_specs=[
                pl.BlockSpec((1, BLK, MEDIA), lambda i, s: (s[i], 0, 0)),
                pl.BlockSpec((MEDIA,), lambda i, s: (0,)),
            ],
            out_specs=pl.BlockSpec((1, BLK, MEDIA), lambda i, s: (i, 0, 0)),
        ),
        out_shape=jax.ShapeDtypeStruct((2, BLK, MEDIA), jnp.bfloat16),
        name="norm_slots",
    )(slots, blocks, media_gain)


def split_words(value):
    high = value.astype(jnp.bfloat16).astype(jnp.float32)
    return high, value - high


def lay_words(lane, head, top, total, extras):
    for k, word in enumerate((*split_words(top), *split_words(total))):
        extras = jnp.where(lane % 8 == 4 * head + k, word, extras)
    return extras


def attend_kernel(
    info_ref, slots_ref, cube_ref, row_ref, col_ref, out_ref, rows, keys, values, numer, state, acc, sem
):
    def copy(b):
        return pltpu.make_async_copy(slots_ref.at[info_ref[b]], rows.at[pl.ds(b * BLK, BLK)], sem.at[b])

    for b in range(BLOCKS):
        copy(b).start()
    wk = cube_ref[:, :288].reshape(MEDIA, COLS)
    wv = cube_ref[:, 288:576].reshape(MEDIA, COLS)
    every = cube_ref[:, 576:].reshape(LAT, COLS)
    acc[...] = jnp.zeros_like(acc)
    for g in range(PARTS):
        for b in range(g * NB, (g + 1) * NB):
            copy(b).wait()
        span = slice(g * FRAME_ROWS, (g + 1) * FRAME_ROWS)
        x = rows[span]
        keys[span] = jnp.dot(x, wk, preferred_element_type=jnp.float32).astype(jnp.bfloat16)
        values[span] = jnp.dot(x, wv, preferred_element_type=jnp.float32).astype(jnp.bfloat16)
    base = info_ref[BLOCKS]
    ends = [info_ref[BLOCKS + 1 + v] for v in range(VIDEOS)]
    offset = lax.broadcasted_iota(jnp.int32, (1, FRAME_ROWS), 1)
    lane = lax.broadcasted_iota(jnp.int32, (NUM_LAT, 128), 1)
    stride = NZ * FRAME_ROWS
    for v in range(VIDEOS):
        first = 0 if v == 0 else ends[v - 1]
        last = ends[v]
        seen = [
            (first < base + g * stride + FRAME_ROWS) & (last > base + g * stride) & (first < last)
            for g in range(PARTS)
        ]

        @pl.when(seen[0] | seen[1] | seen[2] | seen[3])
        def _():
            pick = (
                row_ref[...] == v * NUM_LAT + lax.broadcasted_iota(jnp.int32, (NUM_LAT, LAT), 0)
            ).astype(jnp.bfloat16)
            queries = jnp.dot(pick, every, preferred_element_type=jnp.float32).astype(jnp.bfloat16)
            numer[...] = jnp.zeros_like(numer)
            for h in range(HEADS_HERE):
                state[2 * h] = jnp.full((NUM_LAT, 1), EMPTY, jnp.float32)
                state[2 * h + 1] = jnp.zeros((NUM_LAT, 1), jnp.float32)
            for g in range(PARTS):
                @pl.when(seen[g])
                def _():
                    position = base + g * stride + offset
                    allowed = (position >= first) & (position < last)
                    span = slice(g * FRAME_ROWS, (g + 1) * FRAME_ROWS)
                    for h in range(HEADS_HERE):
                        cols = slice(h * HEAD_DIM, (h + 1) * HEAD_DIM)
                        scores = lax.dot_general(
                            queries[:, cols],
                            keys[span, cols],
                            (((1,), (1,)), ((), ())),
                            preferred_element_type=jnp.float32,
                        ) * SCALE2
                        scores = jnp.where(allowed, scores, EMPTY)
                        before = state[2 * h]
                        high, low = split_words(
                            jnp.maximum(before, jnp.max(scores, axis=1, keepdims=True))
                        )
                        top = high + low.astype(jnp.bfloat16).astype(jnp.float32)
                        weights = jnp.where(allowed, jnp.exp2(scores - top), 0.0)
                        keep = jnp.where(before > EMPTY, jnp.exp2(before - top), 0.0)
                        state[2 * h] = top
                        state[2 * h + 1] = state[2 * h + 1] * keep + jnp.sum(weights, axis=1, keepdims=True)
                        numer[:, cols] = numer[:, cols] * keep + jnp.dot(
                            weights.astype(jnp.bfloat16), values[span, cols], preferred_element_type=jnp.float32
                        )
            put = (
                col_ref[...] == v * NUM_LAT + lax.broadcasted_iota(jnp.int32, (PADDED, NUM_LAT), 1)
            ).astype(jnp.bfloat16)
            extras = jnp.zeros((NUM_LAT, 128), jnp.float32)
            for h in range(HEADS_HERE):
                extras = lay_words(lane, h, state[2 * h], state[2 * h + 1], extras)
            acc[:, :COLS] += jnp.dot(put, numer[...].astype(jnp.bfloat16), preferred_element_type=jnp.float32)
            acc[:, COLS:] += jnp.dot(put, extras.astype(jnp.bfloat16), preferred_element_type=jnp.float32)

    words = acc[:, COLS:].reshape(PADDED // 8, 8, 128)
    row = lax.broadcasted_iota(jnp.int32, words.shape, 1)
    group = lax.broadcasted_iota(jnp.int32, words.shape, 2) // 8
    words = jnp.sum(jnp.where(row == group, words, 0.0), axis=1, keepdims=True)
    sums = acc[:, :128].reshape(PADDED // 8, 8, 128)
    out_ref[:, :128] = jnp.where(row == OWN, words, sums).reshape(PADDED, 128).astype(jnp.bfloat16)
    out_ref[:, 128:] = acc[:, 128:COLS].astype(jnp.bfloat16)


def attend(info, slots, cube, place, target):
    return pl.pallas_call(
        attend_kernel,
        in_specs=[SMEM] + [pl.BlockSpec(memory_space=pl.ANY)] + [VMEM] * 3,
        out_specs=VMEM,
        out_shape=jax.ShapeDtypeStruct((PADDED, COLS), jnp.bfloat16),
        scratch_shapes=[
            pltpu.VMEM((ROWS, MEDIA), jnp.bfloat16),
            pltpu.VMEM((ROWS, COLS), jnp.bfloat16),
            pltpu.VMEM((ROWS, COLS), jnp.bfloat16),
            pltpu.VMEM((NUM_LAT, COLS), jnp.float32),
            pltpu.VMEM((2 * HEADS_HERE, NUM_LAT, 1), jnp.float32),
            pltpu.VMEM((PADDED, COLS + 128), jnp.float32),
            pltpu.SemaphoreType.DMA((BLOCKS,)),
        ],
        compiler_params=pltpu.CompilerParams(vmem_limit_bytes=48 * 1024 * 1024),
        name="attend",
    )(info, slots, cube, place.reshape(1, LAT), target.reshape(PADDED, 1))


def arrange_kernel(rows_ref, out_ref):
    count = NY * NZ * 24
    to = lax.broadcasted_iota(jnp.int32, (count, 1), 0)
    key = jnp.where(to < 288, to, to - 288)
    pair = key // 9 * 24 + key % 9 + jnp.where(to < 288, 0, 9)
    query = to - 576
    pick = jnp.where(to < 576, pair, query // OWN * 24 + query % OWN + 18)
    move = (pick == lax.broadcasted_iota(jnp.int32, (count, count), 1)).astype(jnp.bfloat16)
    rows = jnp.dot(move, rows_ref[...], preferred_element_type=jnp.float32).astype(jnp.bfloat16)
    for i in range(NX):
        out_ref[i] = rows


def arrange(rows):
    return pl.pallas_call(
        arrange_kernel,
        in_specs=[VMEM],
        out_specs=VMEM,
        out_shape=jax.ShapeDtypeStruct((NX, NY * NZ * 24, COLS), jnp.bfloat16),
        compiler_params=pltpu.CompilerParams(vmem_limit_bytes=32 * 1024 * 1024),
        name="arrange",
    )(rows.reshape(NY * NZ * 24, COLS))


def finish_kernel(parts_ref, out_ref):
    shape = (NX, NZ, 8, HEAD_DIM)
    lane = lax.broadcasted_iota(jnp.int32, shape, 3)
    row = lax.broadcasted_iota(jnp.int32, shape, 2)
    for part in range(PARTS):
        words = parts_ref[:, part, :, OWN:OWN + 1, :128].astype(jnp.float32)
        for h in range(HEADS_HERE):
            cols = slice(h * HEAD_DIM, (h + 1) * HEAD_DIM)
            at = lane - (8 * row + 4 * h)
            top = jnp.sum(jnp.where((at == 0) | (at == 1), words, 0.0), axis=3, keepdims=True)
            total = jnp.sum(jnp.where((at == 2) | (at == 3), words, 0.0), axis=3, keepdims=True)
            top = jnp.where(total > 0, top, EMPTY)
            best = jnp.max(top, axis=(0, 1), keepdims=True)
            factor = jnp.where(total > 0, jnp.exp2(top - best), 0.0)
            whole = jnp.sum(total * factor, axis=(0, 1))
            numer = jnp.sum(parts_ref[:, part, :, :, cols].astype(jnp.float32) * factor, axis=(0, 1))
            result = (numer / whole).astype(jnp.bfloat16)
            start = part * COLS + h * HEAD_DIM
            out_ref[:, start:start + HEAD_DIM] = result[:OWN]


def finish(parts):
    return pl.pallas_call(
        finish_kernel,
        in_specs=[VMEM],
        out_specs=VMEM,
        out_shape=jax.ShapeDtypeStruct((OWN, PARTS * COLS), jnp.bfloat16),
        compiler_params=pltpu.CompilerParams(vmem_limit_bytes=48 * 1024 * 1024),
        name="finish",
    )(parts.reshape(NX, NY, NZ, 8, COLS))


def exchange(value, axis):
    return lax.all_to_all(value, axis, split_axis=0, concat_axis=0, tiled=True)


def spread(value, axis, count):
    return exchange(jnp.broadcast_to(value[None], (count,) + value.shape), axis)


def shards(
    encoded,
    block_source,
    block_slot,
    video_patches,
    latent_video,
    media_gain,
    queries,
    w_key,
    w_value,
):
    ax, az = lax.axis_index("x"), lax.axis_index("z")
    al, ac = lax.axis_index("yl"), lax.axis_index("c")
    head = al * 2 + ac
    slot = lax.dynamic_index_in_dim(block_slot[0], head, 0, keepdims=False)[:2]
    own = norm_slots(slot, encoded.reshape(NB, BLK, MEDIA), media_gain)
    slots = lax.all_gather(own, ("yh", "yl", "c"), axis=0, tiled=True)
    local = jnp.concatenate([w_key, w_value, queries], axis=0)
    local = jnp.transpose(local.reshape(24, PARTS, COLS), (1, 0, 2))
    plane = exchange(jnp.repeat(local, NZ, axis=0), ("yh", "z"))
    cube = exchange(arrange(plane), "x")

    source = exchange(jnp.broadcast_to(block_source[None], (NY, NB, 1)), "yh").reshape(BLOCKS)
    block = jnp.arange(BLOCKS, dtype=jnp.int32)
    same = (source[:, None] == source[None, :]) & (block[None, :] < block[:, None])
    same = same & (block[:, None] // NB == block[None, :] // NB)
    rank = jnp.sum(same.astype(jnp.int32), axis=1)
    index = (block // NB * 4 + source) * 2 + rank
    ends = jnp.cumsum(video_patches)
    base = (ax * (NY * NZ) + az) * FRAME_ROWS
    info = jnp.concatenate([index, base[None].astype(jnp.int32), ends.astype(jnp.int32)]).astype(jnp.int32)

    which = (latent_video[:, None] == jnp.arange(VIDEOS)[None, :]).astype(jnp.int32)
    before = jnp.cumsum(which, axis=0) - which
    block_place = latent_video * NUM_LAT + LAT_BLK * jnp.sum(before * which, axis=1)
    place = (block_place[:, None] + jnp.arange(LAT_BLK)[None, :]).reshape(-1).astype(jnp.int32)

    target = jnp.pad(place.reshape(PADDED // 8, OWN), ((0, 0), (0, 8 - OWN)), constant_values=-1)
    message = attend(info, slots, cube, place, target)
    return finish(exchange(message.reshape(PADDED // 8, 8, COLS), ("x", "yh", "z")))


def solution(mesh):
    grid = Mesh(mesh.devices.reshape(NX, NY, NZ, 2, 2), ("x", "yh", "z", "yl", "c"))
    frame, head = ("x", "yh", "z"), ("yl", "c")
    placed = (
        P(frame + head, None),
        P(frame, None),
        P(frame, None, None),
        P(),
        P(),
        P(),
        P(frame, head),
        P(frame, head),
        P(frame, head),
    )
    return jax.shard_map(
        shards, mesh=grid, in_specs=placed, out_specs=P(frame, head), check_vma=False
    )
```

time: 158 us -> 140 us (0.89)
  between operations: 0.28 us -> 13.6 us
  starting transfers between devices: 37.5 us -> 25.6 us
  local copies, waits for them, and re-layouts: 14.9 us -> 4.2 us
  waiting for transfers between devices: 48 us -> 39.3 us
  blocking collectives: 35.2 us -> 37.7 us
  other arithmetic: 4.16 us -> 2.51 us
    ppermute x6 -> x0, waiting for transfers between devices: 15.9 us -> none  [the longest x1 8.22 us: shards(): near_y = lax.ppermute(own, 'yl', swap)]
    ppermute x6 -> x0, starting transfers between devices: 15.4 us -> none  [the longest x1 3.92 us: shards(): source_z = lax.ppermute(block_source, 'z', swap_z)]
    all_gather x0 -> x1, waiting for transfers between devices: none -> 5.53 us  [shards(): slots = lax.all_gather(own, ('yh', 'yl', 'c'), axis=0, tiled=True)]
    unnamed x14 -> x15, local copies, waits for them, and re-layouts: 5.12 us -> 0.77 us
    all_to_all x3, starting transfers between devices: 22.2 us -> 25.6 us  [exchange(): return lax.all_to_all(value, axis, split_axis=0, concat_axis=0, tiled=True)]
    all_to_all x2 -> x1, blocking collectives: 35.2 us -> 37.7 us  [exchange(): return lax.all_to_all(value, axis, split_axis=0, concat_axis=0, tiled=True)]
    slice x9 -> x1, local copies, waits for them, and re-layouts: 2.09 us -> 0.22 us  [the longest x1 0.73 us: shards(): far_y = lax.ppermute(near_z[0:1], 'yl', swap)]
    concatenate x1 -> x0, local copies, waits for them, and re-layouts: 1.69 us -> none  [shards(): mine = jnp.concatenate([own, near_y, near_z, far_y, far_z], axis=0)]
  transfers between devices with their start and end apart: 9 -> 4, of which waited for: 4 -> 4; matrix products, arithmetic and copies ran while one was open for 10% -> 4% of each run, Pallas kernels for 2% -> 1%
where the time goes in v2:
time: 140 us
  waiting for transfers between devices  39.3 us (28%)
  blocking collectives  37.7 us (27%)
  starting transfers between devices  25.6 us (18%)
  Pallas kernels  16.9 us (12%)
  between operations  13.6 us (10%)
  local copies, waits for them, and re-layouts  4.2 us (3%)
  other arithmetic  2.51 us (2%)
    all_to_all x1, blocking collectives, exchange(): return lax.all_to_all(value, axis, split_axis=0, concat_axis=0, tiled=True)  37.7 us
    all_to_all x3, waiting for transfers between devices, exchange(): return lax.all_to_all(value, axis, split_axis=0, concat_axis=0, tiled=True)  33.8 us
    all_to_all x3, starting transfers between devices, exchange(): return lax.all_to_all(value, axis, split_axis=0, concat_axis=0, tiled=True)  25.6 us
    pallas_call x1, Pallas kernels, attend(): pl.pallas_call(attend_kernel, in_specs=[SMEM] + [pl.BlockSpec(memory_spac...  10.8 us
    all_gather x1, waiting for transfers between devices, shards(): slots = lax.all_gather(own, ('yh', 'yl', 'c'), axis=0, tiled=True)  5.53 us
    pallas_call x1, Pallas kernels, norm_slots(): pl.pallas_call(norm_kernel, grid_spec=pltpu.PrefetchScalarGridSpec(num_sc...  3.04 us
  transfers between devices with their start and end apart: 4, of which 4 were waited for; matrix products, arithmetic and copies ran while one was open for 4% of the time, Pallas kernels for 1%

profile of v2, /device:TPU:16, one launch (start us, length us, event | category | flops | bytes accessed | tf_op | source)
XLA Modules:
  0.0 139.9 jit_solution(1833083530690625295)
XLA Ops:
  6.5 0.0 copy-start
  6.5 0.0 copy-start.4
  6.5 0.0 copy-start.1
  6.5 0.0 copy-start.2
  6.5 0.0 all-gather.2.cloned.1.call-start
  6.6 0.6 copy-done
  7.2 0.5 slice_bitcast_fusion.slot_ref
  7.7 0.0 copy-start.6
  7.7 0.0 copy-start.3
  7.7 0.0 copy-start.5
  7.7 3.0 %norm_slots.1 = bf16[2,128,1152]{2,1,0:T(8,128)(2,1)} custom-call(s32[2]{0:T(128)} %slice_bitcast_fusion.slot_ref, bf16[4,128,1152]{2,1,0:T(8,128)(2,1)} %bitcast.38, f32[1152]{0:T(1024)} %gain_ref.1), custom_call_target="tpu_custom_call" | custom-call | tf_op jit(solution)/shard_map/norm_slots/pallas_call | solution.py:43
  10.8 0.0 all-gather.2.cloned.1.call-update
  10.8 0.0 copy-done.4
  10.8 0.0 copy-done.1
  10.8 0.0 copy-done.2
  10.9 0.8 broadcast_in_dim.11
  11.7 16.1 %all-to-all-start.1 = ((bf16[32,24,256]{2,1,0:T(8,128)(2,1)}), bf16[32,24,256]{2,1,0:T(8,128)(2,1)S(1)}, u32[]{:S(2)}, u32[]{:S(2)}) async-start(bf16[32,24,256]{2,1,0:T(8,128)(2,1)} %bitcast.7), calls=%async_computation.1 | async-start | bytes 786432 | tf_op jit(solution)/shard_map/all_to_all | solution.py:234
  27.8 0.0 copy-done.6
  27.8 0.2 reduce-window.19
  28.0 0.0 copy-done.3
  28.0 0.9 reduce-window.20
  28.9 0.2 slice_reduce_fusion
  29.1 0.2 reduce-window.21
  29.3 0.1 add_bitcast_fusion
  29.4 16.5 %all-to-all-done.1 = bf16[32,24,256]{2,1,0:T(8,128)(2,1)S(1)} async-done(((bf16[32,24,256]{2,1,0:T(8,128)(2,1)}), bf16[32,24,256]{2,1,0:T(8,128)(2,1)S(1)}, u32[]{:S(2)}, u32[]{:S(2)}) %all-to-all-start.1) | async-done | bytes 393248 | tf_op jit(solution)/shard_map/all_to_all | solution.py:234
  45.9 0.0 copy-done.5
  45.9 0.6 broadcast_in_dim.9
  46.4 5.2 %all-to-all-start = ((s32[4,4,1]{1,2,0:T(1,128)}), s32[4,4,1]{1,2,0:T(1,128)S(1)}, u32[]{:S(2)}, u32[]{:S(2)}) async-start(s32[4,4,1]{1,2,0:T(1,128)} %broadcast_in_dim.9), calls=%async_computation | async-start | bytes 4096 | tf_op jit(solution)/shard_map/all_to_all | solution.py:234
  51.6 1.7 %arrange.1 = bf16[4,768,256]{2,1,0:T(8,128)(2,1)} custom-call(bf16[768,256]{1,0:T(8,128)(2,1)S(1)} %bitcast.37), custom_call_target="tpu_custom_call" | custom-call | tf_op jit(solution)/shard_map/arrange/pallas_call | solution.py:191
  53.3 3.5 %all-to-all-done = s32[4,4,1]{1,2,0:T(1,128)S(1)} async-done(((s32[4,4,1]{1,2,0:T(1,128)}), s32[4,4,1]{1,2,0:T(1,128)S(1)}, u32[]{:S(2)}, u32[]{:S(2)}) %all-to-all-start) | async-done | bytes 96 | tf_op jit(solution)/shard_map/all_to_all | solution.py:234
  56.8 4.3 %all-to-all-start.2 = ((bf16[4,768,256]{2,1,0:T(8,128)(2,1)}), bf16[4,768,256]{2,1,0:T(8,128)(2,1)S(1)}, u32[]{:S(2)}, u32[]{:S(2)}) async-start(bf16[4,768,256]{2,1,0:T(8,128)(2,1)} %arrange.1), calls=%async_computation.2 | async-start | bytes 3145728 | tf_op jit(solution)/shard_map/all_to_all | solution.py:234
  61.2 0.2 add.82
  61.4 0.1 iota_add_fusion
  61.5 0.2 add.81.row_ref
  61.7 0.1 copy.20
  61.8 0.1 add.86
  61.9 0.1 broadcast_add_fusion
  61.9 0.1 copy.23
  62.1 0.2 reshape.185.col_ref
  62.3 0.5 broadcast.127
  62.8 0.6 reduce.5
  63.4 0.1 reshape.174
  63.5 0.2 convert_reduce_fusion
  63.7 0.1 pad_add_fusion.info_ref
  63.8 13.8 %all-to-all-done.2.cube_ref = bf16[4,768,256]{2,1,0:T(8,128)(2,1)S(1)} async-done(((bf16[4,768,256]{2,1,0:T(8,128)(2,1)}), bf16[4,768,256]{2,1,0:T(8,128)(2,1)S(1)}, u32[]{:S(2)}, u32[]{:S(2)}) %all-to-all-start.2) | async-done | bytes 1572896 | tf_op jit(solution)/shard_map/all_to_all | solution.py:234
  77.5 5.5 %all-gather.2.cloned.1.call-done.slots_ref = bf16[32,128,1152]{2,1,0:T(8,128)(2,1)} async-done(((bf16[2,128,1152]{2,1,0:T(8,128)(2,1)}), bf16[32,128,1152]{2,1,0:T(8,128)(2,1)}) %all-gather.2.cloned.1.call-update) | async-done | bytes 9437200 | tf_op jit(solution)/shard_map/all_gather | solution.py:257
  83.1 10.8 %attend.1 = bf16[1024,256]{1,0:T(8,128)(2,1)S(1)} custom-call(s32[20]{0:T(128)S(1)} %pad_add_fusion.info_ref, bf16[32,128,1152]{2,1,0:T(8,128)(2,1)} %all-gather.2.cloned.1.call-done.slots_ref, bf16[4,768,256]{2,1,0:T(8,128)(2,1)S(1)} %all-to-all-done.2.cube_ref, s32[1,768]{1,0:T(1,128)S(1)} %add.81.row_ref, s32[1024,1]{1,0:T(8,128)S(1)} %reshape.185.col_ref), custom_call_target="tpu_custom_call" | custom-call | tf_op jit(solution)/shard_map/attend/pallas_call | solution.py:158
  93.9 37.7 %all_to_all.20 = bf16[128,8,256]{2,1,0:T(8,128)(2,1)S(1)} all-to-all(bf16[128,8,256]{2,1,0:T(8,128)(2,1)S(1)} %bitcast.36), channel_id=1, replica_groups=mesh['x'=4,'yh'=4,'z'=8,'yl'=2,'c'=2] {'x','yh','z'}, dimensions={0} | all-to-all | bytes 1048576 | tf_op jit(solution)/shard_map/all_to_all | solution.py:234
  131.7 1.3 finish.1
  (13 shorter events, 0.1 us)
Async XLA Ops:
  6.5 0.7 copy-start
  6.5 4.3 %copy-start.4 = (bf16[6,1024]{1,0:T(8,128)(2,1)S(1)}, bf16[6,1024]{1,0:T(8,128)(2,1)}, u32[]{:S(2)}) copy-start(bf16[6,1024]{1,0:T(8,128)(2,1)} %param.15) | copy-start | bytes 36868
  6.5 4.3 %copy-start.1 = (bf16[9,1024]{1,0:T(8,128)(2,1)S(1)}, bf16[9,1024]{1,0:T(8,128)(2,1)}, u32[]{:S(2)}) copy-start(bf16[9,1024]{1,0:T(8,128)(2,1)} %param.17) | copy-start | bytes 55300
  6.5 4.3 %copy-start.2 = (bf16[9,1024]{1,0:T(8,128)(2,1)S(1)}, bf16[9,1024]{1,0:T(8,128)(2,1)}, u32[]{:S(2)}) copy-start(bf16[9,1024]{1,0:T(8,128)(2,1)} %param.16) | copy-start | bytes 55300
  6.5 76.5 %all-gather.2.cloned.1.call-start = ((), (), s32[]{:S(2)}) async-start(), calls=%async_computation.4 | async-start | bytes 10027008 | tf_op jit(solution)/shard_map/all_gather | solution.py:257
  7.7 20.0 %copy-start.6 = (s32[3]{0:T(128)S(1)}, s32[3]{0:T(128)}, u32[]{:S(2)}) copy-start(s32[3]{0:T(128)} %param.12) | copy-start | bytes 40
  7.7 20.2 %copy-start.3 = (s32[384]{0:T(512)S(1)}, s32[384]{0:T(512)}, u32[]{:S(2)}) copy-start(s32[384]{0:T(512)} %param.13) | copy-start | bytes 4612
  7.7 38.1 %copy-start.5 = (s32[4,1]{0,1:T(1,128)S(1)}, s32[4,1]{0,1:T(1,128)}, u32[]{:S(2)}) copy-start(s32[4,1]{0,1:T(1,128)} %param.10) | copy-start | bytes 52
  11.7 34.2 %all-to-all-start.1 = ((bf16[32,24,256]{2,1,0:T(8,128)(2,1)}), bf16[32,24,256]{2,1,0:T(8,128)(2,1)S(1)}, u32[]{:S(2)}, u32[]{:S(2)}) async-start(bf16[32,24,256]{2,1,0:T(8,128)(2,1)} %bitcast.7), calls=%async_computation.1 | async-start | bytes 786432 | tf_op jit(solution)/shard_map/all_to_all | solution.py:234
  46.4 10.4 %all-to-all-start = ((s32[4,4,1]{1,2,0:T(1,128)}), s32[4,4,1]{1,2,0:T(1,128)S(1)}, u32[]{:S(2)}, u32[]{:S(2)}) async-start(s32[4,4,1]{1,2,0:T(1,128)} %broadcast_in_dim.9), calls=%async_computation | async-start | bytes 4096 | tf_op jit(solution)/shard_map/all_to_all | solution.py:234
  56.8 20.7 %all-to-all-start.2 = ((bf16[4,768,256]{2,1,0:T(8,128)(2,1)}), bf16[4,768,256]{2,1,0:T(8,128)(2,1)S(1)}, u32[]{:S(2)}, u32[]{:S(2)}) async-start(bf16[4,768,256]{2,1,0:T(8,128)(2,1)} %arrange.1), calls=%async_computation.2 | async-start | bytes 3145728 | tf_op jit(solution)/shard_map/all_to_all | solution.py:234
Sparse Core Ops, SparseCore 0:
  10.9 72.1 all-gather.1

commit v3 on v2

--- a/solution.py
+++ b/solution.py
@@ -178,9 +178,10 @@
     count = NY * NZ * 24
     to = lax.broadcasted_iota(jnp.int32, (count, 1), 0)
     key = jnp.where(to < 288, to, to - 288)
-    pair = key // 9 * 24 + key % 9 + jnp.where(to < 288, 0, 9)
     query = to - 576
-    pick = jnp.where(to < 576, pair, query // OWN * 24 + query % OWN + 18)
+    frame = jnp.where(to < 576, key // 9, query // OWN)
+    row = jnp.where(to < 576, key % 9 + jnp.where(to < 288, 0, 9), query % OWN + 18)
+    pick = (frame % NZ * NY + frame // NZ) * 24 + row
     move = (pick == lax.broadcasted_iota(jnp.int32, (count, count), 1)).astype(jnp.bfloat16)
     rows = jnp.dot(move, rows_ref[...], preferred_element_type=jnp.float32).astype(jnp.bfloat16)
     for i in range(NX):
@@ -257,10 +258,12 @@
     slots = lax.all_gather(own, ("yh", "yl", "c"), axis=0, tiled=True)
     local = jnp.concatenate([w_key, w_value, queries], axis=0)
     local = jnp.transpose(local.reshape(24, PARTS, COLS), (1, 0, 2))
-    plane = exchange(jnp.repeat(local, NZ, axis=0), ("yh", "z"))
-    cube = exchange(arrange(plane), "x")
-
-    source = exchange(jnp.broadcast_to(block_source[None], (NY, NB, 1)), "yh").reshape(BLOCKS)
+    note = jnp.pad(block_source.reshape(1, NB).astype(jnp.bfloat16), ((0, 7), (0, COLS - NB)))
+    local = jnp.concatenate([local, jnp.broadcast_to(note[None], (PARTS, 8, COLS))], axis=1)
+    column = exchange(local, "yh")
+    cube = exchange(arrange(spread(column[:, :24], "z", NZ)), "x")
+
+    source = column[:, 24, :NB].astype(jnp.int32).reshape(BLOCKS)
     block = jnp.arange(BLOCKS, dtype=jnp.int32)
     same = (source[:, None] == source[None, :]) & (block[None, :] < block[:, None])
     same = same & (block[:, None] // NB == block[None, :] // NB)

time: 140 us -> 135 us (0.964)
  the two profiles are of different devices: /device:TPU:16 before, /device:TPU:8 now
where the time goes in v3:
time: 135 us; the launch traced here: 134 us
  blocking collectives  52.3 us (39%)
  waiting for transfers between devices  31.3 us (23%)
  Pallas kernels  17.1 us (13%)
  starting transfers between devices  14.9 us (11%)
  between operations  13.6 us (10%)
  local copies, waits for them, and re-layouts  3.11 us (2%)
  other arithmetic  1.96 us (1%)
    all_to_all x2, blocking collectives, exchange(): return lax.all_to_all(value, axis, split_axis=0, concat_axis=0, tiled=True)  52.3 us
    all_to_all x2, waiting for transfers between devices, exchange(): return lax.all_to_all(value, axis, split_axis=0, concat_axis=0, tiled=True)  27.9 us
    all_to_all x2, starting transfers between devices, exchange(): return lax.all_to_all(value, axis, split_axis=0, concat_axis=0, tiled=True)  14.9 us
    pallas_call x1, Pallas kernels, attend(): pl.pallas_call(attend_kernel, in_specs=[SMEM] + [pl.BlockSpec(memory_spac...  10.8 us
    all_gather x1, waiting for transfers between devices, shards(): slots = lax.all_gather(own, ('yh', 'yl', 'c'), axis=0, tiled=True)  3.41 us
    pallas_call x1, Pallas kernels, norm_slots(): pl.pallas_call(norm_kernel, grid_spec=pltpu.PrefetchScalarGridSpec(num_sc...  2.91 us
  transfers between devices with their start and end apart: 3, of which 3 were waited for; matrix products, arithmetic and copies ran while one was open for 3% of the time, Pallas kernels for 2%

profile of v3, /device:TPU:8, one launch (start us, length us, event | category | flops | bytes accessed | tf_op | source)
XLA Modules:
  0.0 134.3 jit_solution(8235471773618565150)
XLA Ops:
  6.5 0.0 copy-start
  6.5 0.0 copy-start.4
  6.5 0.0 copy-start.1
  6.5 0.0 copy-start.2
  6.5 0.0 copy-start.5
  6.5 0.0 all-gather.2.cloned.1.call-start
  6.6 0.6 copy-done
  7.2 0.5 slice_bitcast_fusion.slot_ref
  7.7 2.9 %norm_slots.1 = bf16[2,128,1152]{2,1,0:T(8,128)(2,1)} custom-call(s32[2]{0:T(128)} %slice_bitcast_fusion.slot_ref, bf16[4,128,1152]{2,1,0:T(8,128)(2,1)} %bitcast.37, f32[1152]{0:T(1024)} %gain_ref.1), custom_call_target="tpu_custom_call" | custom-call | tf_op jit(solution)/shard_map/norm_slots/pallas_call | solution.py:43
  10.6 0.0 copy-start.3
  10.7 0.0 all-gather.2.cloned.1.call-update
  10.7 0.0 copy-done.4
  10.7 0.0 copy-done.1
  10.7 0.0 copy-done.2
  10.8 0.0 copy-done.5
  10.9 14.1 %all_to_all.20 = bf16[4,32,256]{2,1,0:T(8,128)(2,1)S(1)} all-to-all(bf16[4,32,256]{2,1,0:T(8,128)(2,1)S(1)} %copy.22), channel_id=1, replica_groups=mesh['x'=4,'yh'=4,'z'=8,'yl'=2,'c'=2] {'yh'}, dimensions={0} | all-to-all | bytes 131072 | tf_op jit(solution)/shard_map/all_to_all | solution.py:235
  25.0 0.8 broadcast_in_dim.8
  25.8 10.4 %all-to-all-start.1 = ((bf16[8,4,24,256]{3,2,1,0:T(8,128)(2,1)}), bf16[8,4,24,256]{3,2,1,0:T(8,128)(2,1)S(1)}, u32[]{:S(2)}, u32[]{:S(2)}) async-start(bf16[8,4,24,256]{3,2,1,0:T(8,128)(2,1)} %broadcast_in_dim.8), calls=%async_computation.1 | async-start | bytes 786432 | tf_op jit(solution)/shard_map/all_to_all | solution.py:235
  36.3 0.0 copy-done.3
  36.3 0.9 reduce-window.20
  37.2 0.2 slice_reduce_fusion
  37.4 0.2 reduce-window.21
  37.6 0.1 add_bitcast_fusion
  37.7 11.8 %all-to-all-done.1 = bf16[8,4,24,256]{3,2,1,0:T(8,128)(2,1)S(1)} async-done(((bf16[8,4,24,256]{3,2,1,0:T(8,128)(2,1)}), bf16[8,4,24,256]{3,2,1,0:T(8,128)(2,1)S(1)}, u32[]{:S(2)}, u32[]{:S(2)}) %all-to-all-start.1) | async-done | bytes 393248 | tf_op jit(solution)/shard_map/all_to_all | solution.py:235
  49.5 2.0 %arrange.1 = bf16[4,768,256]{2,1,0:T(8,128)(2,1)} custom-call(bf16[768,256]{1,0:T(8,128)(2,1)S(1)} %bitcast.36), custom_call_target="tpu_custom_call" | custom-call | tf_op jit(solution)/shard_map/arrange/pallas_call | solution.py:192
  51.5 0.0 copy-start.6
  51.5 4.4 %all-to-all-start.2 = ((bf16[4,768,256]{2,1,0:T(8,128)(2,1)}), bf16[4,768,256]{2,1,0:T(8,128)(2,1)S(1)}, u32[]{:S(2)}, u32[]{:S(2)}) async-start(bf16[4,768,256]{2,1,0:T(8,128)(2,1)} %arrange.1), calls=%async_computation.2 | async-start | bytes 3145728 | tf_op jit(solution)/shard_map/all_to_all | solution.py:235
  56.0 0.0 copy-done.6
  56.0 0.2 reduce-window.19
  56.2 0.2 add.84
  56.4 0.1 iota_add_fusion
  56.5 0.2 add.83.row_ref
  56.6 0.1 copy.23
  56.7 0.1 add.88
  56.8 0.1 broadcast_add_fusion
  56.9 0.1 copy.26
  57.0 0.2 reshape.203.col_ref
  57.3 0.1 reshape.202
  57.3 0.2 convert_reduce_fusion
  57.5 0.1 pad_add_fusion.info_ref
  57.6 16.1 %all-to-all-done.2.cube_ref = bf16[4,768,256]{2,1,0:T(8,128)(2,1)S(1)} async-done(((bf16[4,768,256]{2,1,0:T(8,128)(2,1)}), bf16[4,768,256]{2,1,0:T(8,128)(2,1)S(1)}, u32[]{:S(2)}, u32[]{:S(2)}) %all-to-all-start.2) | async-done | bytes 1572896 | tf_op jit(solution)/shard_map/all_to_all | solution.py:235
  73.7 3.4 %all-gather.2.cloned.1.call-done.slots_ref = bf16[32,128,1152]{2,1,0:T(8,128)(2,1)} async-done(((bf16[2,128,1152]{2,1,0:T(8,128)(2,1)}), bf16[32,128,1152]{2,1,0:T(8,128)(2,1)}) %all-gather.2.cloned.1.call-update) | async-done | bytes 9437200 | tf_op jit(solution)/shard_map/all_gather | solution.py:258
  77.1 10.8 %attend.1 = bf16[1024,256]{1,0:T(8,128)(2,1)S(1)} custom-call(s32[20]{0:T(128)S(1)} %pad_add_fusion.info_ref, bf16[32,128,1152]{2,1,0:T(8,128)(2,1)} %all-gather.2.cloned.1.call-done.slots_ref, bf16[4,768,256]{2,1,0:T(8,128)(2,1)S(1)} %all-to-all-done.2.cube_ref, s32[1,768]{1,0:T(1,128)S(1)} %add.83.row_ref, s32[1024,1]{1,0:T(8,128)S(1)} %reshape.203.col_ref), custom_call_target="tpu_custom_call" | custom-call | tf_op jit(solution)/shard_map/attend/pallas_call | solution.py:158
  88.0 38.2 %all_to_all.21 = bf16[128,8,256]{2,1,0:T(8,128)(2,1)S(1)} all-to-all(bf16[128,8,256]{2,1,0:T(8,128)(2,1)S(1)} %bitcast.35), channel_id=1, replica_groups=mesh['x'=4,'yh'=4,'z'=8,'yl'=2,'c'=2] {'x','yh','z'}, dimensions={0} | all-to-all | bytes 1048576 | tf_op jit(solution)/shard_map/all_to_all | solution.py:235
  126.2 1.3 finish.1
  (19 shorter events, 0.2 us)
Async XLA Ops:
  6.5 0.7 copy-start
  6.5 4.1 %copy-start.4 = (bf16[6,1024]{1,0:T(8,128)(2,1)S(1)}, bf16[6,1024]{1,0:T(8,128)(2,1)}, u32[]{:S(2)}) copy-start(bf16[6,1024]{1,0:T(8,128)(2,1)} %param.15) | copy-start | bytes 36868
  6.5 4.1 %copy-start.1 = (bf16[9,1024]{1,0:T(8,128)(2,1)S(1)}, bf16[9,1024]{1,0:T(8,128)(2,1)}, u32[]{:S(2)}) copy-start(bf16[9,1024]{1,0:T(8,128)(2,1)} %param.17) | copy-start | bytes 55300
  6.5 4.2 %copy-start.2 = (bf16[9,1024]{1,0:T(8,128)(2,1)S(1)}, bf16[9,1024]{1,0:T(8,128)(2,1)}, u32[]{:S(2)}) copy-start(bf16[9,1024]{1,0:T(8,128)(2,1)} %param.16) | copy-start | bytes 55300
  6.5 4.2 %copy-start.5 = (s32[4,1]{0,1:T(1,128)S(1)}, s32[4,1]{0,1:T(1,128)}, u32[]{:S(2)}) copy-start(s32[4,1]{0,1:T(1,128)} %param.10) | copy-start | bytes 52
  6.5 70.6 %all-gather.2.cloned.1.call-start = ((), (), s32[]{:S(2)}) async-start(), calls=%async_computation.4 | async-start | bytes 10027008 | tf_op jit(solution)/shard_map/all_gather | solution.py:258
  10.6 25.6 %copy-start.3 = (s32[384]{0:T(512)S(1)}, s32[384]{0:T(512)}, u32[]{:S(2)}) copy-start(s32[384]{0:T(512)} %param.13) | copy-start | bytes 4612
  25.8 23.7 %all-to-all-start.1 = ((bf16[8,4,24,256]{3,2,1,0:T(8,128)(2,1)}), bf16[8,4,24,256]{3,2,1,0:T(8,128)(2,1)S(1)}, u32[]{:S(2)}, u32[]{:S(2)}) async-start(bf16[8,4,24,256]{3,2,1,0:T(8,128)(2,1)} %broadcast_in_dim.8), calls=%async_computation.1 | async-start | bytes 786432 | tf_op jit(solution)/shard_map/all_to_all | solution.py:235
  51.5 4.4 %copy-start.6 = (s32[3]{0:T(128)S(1)}, s32[3]{0:T(128)}, u32[]{:S(2)}) copy-start(s32[3]{0:T(128)} %param.12) | copy-start | bytes 40
  51.5 22.2 %all-to-all-start.2 = ((bf16[4,768,256]{2,1,0:T(8,128)(2,1)}), bf16[4,768,256]{2,1,0:T(8,128)(2,1)S(1)}, u32[]{:S(2)}, u32[]{:S(2)}) async-start(bf16[4,768,256]{2,1,0:T(8,128)(2,1)} %arrange.1), calls=%async_computation.2 | async-start | bytes 3145728 | tf_op jit(solution)/shard_map/all_to_all | solution.py:235
Sparse Core Ops, SparseCore 0:
  10.8 66.2 all-gather.1

commit v4 on v3

--- a/solution.py
+++ b/solution.py
@@ -32,11 +32,12 @@
 SMEM = pl.BlockSpec(memory_space=pltpu.SMEM)
 
 
-def norm_kernel(slot_ref, rows_ref, gain_ref, out_ref):
-    values = rows_ref[0].astype(jnp.float32)
-    center = values - jnp.mean(values, axis=1, keepdims=True)
-    spread = jnp.mean(center * center, axis=1, keepdims=True)
-    out_ref[0] = (center * lax.rsqrt(spread + 1e-6) * gain_ref[...][None, :]).astype(jnp.bfloat16)
+def norm_kernel(slot_ref, first_ref, second_ref, gain_ref, out_ref):
+    for i, rows_ref in enumerate((first_ref, second_ref)):
+        values = rows_ref[0].astype(jnp.float32)
+        center = values - jnp.mean(values, axis=1, keepdims=True)
+        spread = jnp.mean(center * center, axis=1, keepdims=True)
+        out_ref[i] = (center * lax.rsqrt(spread + 1e-6) * gain_ref[...][None, :]).astype(jnp.bfloat16)
 
 
 def norm_slots(slots, blocks, media_gain):
@@ -44,16 +45,17 @@
         norm_kernel,
         grid_spec=pltpu.PrefetchScalarGridSpec(
             num_scalar_prefetch=1,
-            grid=(2,),
+            grid=(1,),
             in_specs=[
-                pl.BlockSpec((1, BLK, MEDIA), lambda i, s: (s[i], 0, 0)),
+                pl.BlockSpec((1, BLK, MEDIA), lambda i, s: (s[0], 0, 0)),
+                pl.BlockSpec((1, BLK, MEDIA), lambda i, s: (s[1], 0, 0)),
                 pl.BlockSpec((MEDIA,), lambda i, s: (0,)),
             ],
-            out_specs=pl.BlockSpec((1, BLK, MEDIA), lambda i, s: (i, 0, 0)),
+            out_specs=pl.BlockSpec((2, BLK, MEDIA), lambda i, s: (0, 0, 0)),
         ),
         out_shape=jax.ShapeDtypeStruct((2, BLK, MEDIA), jnp.bfloat16),
         name="norm_slots",
-    )(slots, blocks, media_gain)
+    )(slots, blocks, blocks, media_gain)
 
 
 def split_words(value):

time: 135 us -> 136 us (level)
  transfers between devices with their start and end apart: 3 -> 3, of which waited for: 3 -> 3; matrix products, arithmetic and copies ran while one was open for 3% -> 3% of each run, Pallas kernels for 2% -> 1%
where the time goes in v4:
time: 136 us; the launch traced here: 135 us
  blocking collectives  53.1 us (39%)
  waiting for transfers between devices  31.3 us (23%)
  Pallas kernels  17.3 us (13%)
  starting transfers between devices  14.9 us (11%)
  between operations  13.6 us (10%)
  local copies, waits for them, and re-layouts  3.17 us (2%)
  other arithmetic  1.96 us (1%)
    all_to_all x2, blocking collectives, exchange(): return lax.all_to_all(value, axis, split_axis=0, concat_axis=0, tiled=True)  53.1 us
    all_to_all x2, waiting for transfers between devices, exchange(): return lax.all_to_all(value, axis, split_axis=0, concat_axis=0, tiled=True)  27.9 us
    all_to_all x2, starting transfers between devices, exchange(): return lax.all_to_all(value, axis, split_axis=0, concat_axis=0, tiled=True)  14.9 us
    pallas_call x1, Pallas kernels, attend(): pl.pallas_call(attend_kernel, in_specs=[SMEM] + [pl.BlockSpec(memory_spac...  10.8 us
    all_gather x1, waiting for transfers between devices, shards(): slots = lax.all_gather(own, ('yh', 'yl', 'c'), axis=0, tiled=True)  3.42 us
    pallas_call x1, Pallas kernels, norm_slots(): pl.pallas_call(norm_kernel, grid_spec=pltpu.PrefetchScalarGridSpec(num_sc...  3.06 us
  transfers between devices with their start and end apart: 3, of which 3 were waited for; matrix products, arithmetic and copies ran while one was open for 3% of the time, Pallas kernels for 1%

profile of v4, /device:TPU:8, one launch (start us, length us, event | category | flops | bytes accessed | tf_op | source)
XLA Modules:
  0.0 135.2 jit_solution(826655096649443350)
XLA Ops:
  6.5 0.0 copy-start
  6.5 0.0 all-gather.2.cloned.1.call-start
  6.5 0.7 copy-done
  7.2 0.5 slice_bitcast_fusion.slot_ref
  7.7 0.0 copy-start.1
  7.7 0.0 copy-start.2
  7.7 0.0 copy-start.4
  7.7 0.0 copy-start.5
  7.7 3.1 %norm_slots.1 = bf16[2,128,1152]{2,1,0:T(8,128)(2,1)} custom-call(s32[2]{0:T(128)} %slice_bitcast_fusion.slot_ref, bf16[4,128,1152]{2,1,0:T(8,128)(2,1)} %bitcast.37, bf16[4,128,1152]{2,1,0:T(8,128)(2,1)} %bitcast.38, f32[1152]{0:T(1024)} %gain_ref.1), custom_call_target="tpu_custom_call" | custom-call | tf_op jit(solution)/shard_map/norm_slots/pallas_call | solution.py:44
  10.8 0.0 copy-start.3
  10.8 0.0 all-gather.2.cloned.1.call-update
  10.8 0.0 copy-done.1
  10.8 0.0 copy-done.2
  10.9 0.0 copy-done.4
  10.9 0.0 copy-done.5
  11.1 14.1 %all_to_all.20 = bf16[4,32,256]{2,1,0:T(8,128)(2,1)S(1)} all-to-all(bf16[4,32,256]{2,1,0:T(8,128)(2,1)S(1)} %copy.22), channel_id=1, replica_groups=mesh['x'=4,'yh'=4,'z'=8,'yl'=2,'c'=2] {'yh'}, dimensions={0} | all-to-all | bytes 131072 | tf_op jit(solution)/shard_map/all_to_all | solution.py:237
  25.2 0.8 broadcast_in_dim.8
  26.0 10.4 %all-to-all-start.1 = ((bf16[8,4,24,256]{3,2,1,0:T(8,128)(2,1)}), bf16[8,4,24,256]{3,2,1,0:T(8,128)(2,1)S(1)}, u32[]{:S(2)}, u32[]{:S(2)}) async-start(bf16[8,4,24,256]{3,2,1,0:T(8,128)(2,1)} %broadcast_in_dim.8), calls=%async_computation.1 | async-start | bytes 786432 | tf_op jit(solution)/shard_map/all_to_all | solution.py:237
  36.4 0.0 copy-done.3
  36.4 0.9 reduce-window.20
  37.4 0.2 slice_reduce_fusion
  37.6 0.2 reduce-window.21
  37.8 0.1 add_bitcast_fusion
  37.9 11.8 %all-to-all-done.1 = bf16[8,4,24,256]{3,2,1,0:T(8,128)(2,1)S(1)} async-done(((bf16[8,4,24,256]{3,2,1,0:T(8,128)(2,1)}), bf16[8,4,24,256]{3,2,1,0:T(8,128)(2,1)S(1)}, u32[]{:S(2)}, u32[]{:S(2)}) %all-to-all-start.1) | async-done | bytes 393248 | tf_op jit(solution)/shard_map/all_to_all | solution.py:237
  49.7 2.0 %arrange.1 = bf16[4,768,256]{2,1,0:T(8,128)(2,1)} custom-call(bf16[768,256]{1,0:T(8,128)(2,1)S(1)} %bitcast.36), custom_call_target="tpu_custom_call" | custom-call | tf_op jit(solution)/shard_map/arrange/pallas_call | solution.py:194
  51.7 0.0 copy-start.6
  51.7 4.4 %all-to-all-start.2 = ((bf16[4,768,256]{2,1,0:T(8,128)(2,1)}), bf16[4,768,256]{2,1,0:T(8,128)(2,1)S(1)}, u32[]{:S(2)}, u32[]{:S(2)}) async-start(bf16[4,768,256]{2,1,0:T(8,128)(2,1)} %arrange.1), calls=%async_computation.2 | async-start | bytes 3145728 | tf_op jit(solution)/shard_map/all_to_all | solution.py:237
  56.1 0.0 copy-done.6
  56.1 0.2 reduce-window.19
  56.3 0.2 add.84
  56.5 0.1 iota_add_fusion
  56.6 0.2 add.83.row_ref
  56.8 0.1 copy.23
  56.9 0.1 add.88
  57.0 0.1 broadcast_add_fusion
  57.0 0.1 copy.26
  57.2 0.2 reshape.203.col_ref
  57.4 0.1 reshape.202
  57.5 0.2 convert_reduce_fusion
  57.7 0.1 pad_add_fusion.info_ref
  57.8 16.1 %all-to-all-done.2.cube_ref = bf16[4,768,256]{2,1,0:T(8,128)(2,1)S(1)} async-done(((bf16[4,768,256]{2,1,0:T(8,128)(2,1)}), bf16[4,768,256]{2,1,0:T(8,128)(2,1)S(1)}, u32[]{:S(2)}, u32[]{:S(2)}) %all-to-all-start.2) | async-done | bytes 1572896 | tf_op jit(solution)/shard_map/all_to_all | solution.py:237
  73.9 3.4 %all-gather.2.cloned.1.call-done.slots_ref = bf16[32,128,1152]{2,1,0:T(8,128)(2,1)} async-done(((bf16[2,128,1152]{2,1,0:T(8,128)(2,1)}), bf16[32,128,1152]{2,1,0:T(8,128)(2,1)}) %all-gather.2.cloned.1.call-update) | async-done | bytes 9437200 | tf_op jit(solution)/shard_map/all_gather | solution.py:260
  77.3 10.8 %attend.1 = bf16[1024,256]{1,0:T(8,128)(2,1)S(1)} custom-call(s32[20]{0:T(128)S(1)} %pad_add_fusion.info_ref, bf16[32,128,1152]{2,1,0:T(8,128)(2,1)} %all-gather.2.cloned.1.call-done.slots_ref, bf16[4,768,256]{2,1,0:T(8,128)(2,1)S(1)} %all-to-all-done.2.cube_ref, s32[1,768]{1,0:T(1,128)S(1)} %add.83.row_ref, s32[1024,1]{1,0:T(8,128)S(1)} %reshape.203.col_ref), custom_call_target="tpu_custom_call" | custom-call | tf_op jit(solution)/shard_map/attend/pallas_call | solution.py:160
  88.1 38.9 %all_to_all.21 = bf16[128,8,256]{2,1,0:T(8,128)(2,1)S(1)} all-to-all(bf16[128,8,256]{2,1,0:T(8,128)(2,1)S(1)} %bitcast.35), channel_id=1, replica_groups=mesh['x'=4,'yh'=4,'z'=8,'yl'=2,'c'=2] {'x','yh','z'}, dimensions={0} | all-to-all | bytes 1048576 | tf_op jit(solution)/shard_map/all_to_all | solution.py:237
  127.1 1.3 finish.1
  (19 shorter events, 0.2 us)
Async XLA Ops:
  6.5 0.7 copy-start
  6.5 70.7 %all-gather.2.cloned.1.call-start = ((), (), s32[]{:S(2)}) async-start(), calls=%async_computation.4 | async-start | bytes 10027008 | tf_op jit(solution)/shard_map/all_gather | solution.py:260
  7.7 3.1 %copy-start.1 = (bf16[9,1024]{1,0:T(8,128)(2,1)S(1)}, bf16[9,1024]{1,0:T(8,128)(2,1)}, u32[]{:S(2)}) copy-start(bf16[9,1024]{1,0:T(8,128)(2,1)} %param.17) | copy-start | bytes 55300
  7.7 3.1 %copy-start.2 = (bf16[9,1024]{1,0:T(8,128)(2,1)S(1)}, bf16[9,1024]{1,0:T(8,128)(2,1)}, u32[]{:S(2)}) copy-start(bf16[9,1024]{1,0:T(8,128)(2,1)} %param.16) | copy-start | bytes 55300
  7.7 3.1 %copy-start.4 = (bf16[6,1024]{1,0:T(8,128)(2,1)S(1)}, bf16[6,1024]{1,0:T(8,128)(2,1)}, u32[]{:S(2)}) copy-start(bf16[6,1024]{1,0:T(8,128)(2,1)} %param.15) | copy-start | bytes 36868
  7.7 3.2 %copy-start.5 = (s32[4,1]{0,1:T(1,128)S(1)}, s32[4,1]{0,1:T(1,128)}, u32[]{:S(2)}) copy-start(s32[4,1]{0,1:T(1,128)} %param.10) | copy-start | bytes 52
  10.8 25.6 %copy-start.3 = (s32[384]{0:T(512)S(1)}, s32[384]{0:T(512)}, u32[]{:S(2)}) copy-start(s32[384]{0:T(512)} %param.13) | copy-start | bytes 4612
  26.0 23.7 %all-to-all-start.1 = ((bf16[8,4,24,256]{3,2,1,0:T(8,128)(2,1)}), bf16[8,4,24,256]{3,2,1,0:T(8,128)(2,1)S(1)}, u32[]{:S(2)}, u32[]{:S(2)}) async-start(bf16[8,4,24,256]{3,2,1,0:T(8,128)(2,1)} %broadcast_in_dim.8), calls=%async_computation.1 | async-start | bytes 786432 | tf_op jit(solution)/shard_map/all_to_all | solution.py:237
  51.7 4.4 %copy-start.6 = (s32[3]{0:T(128)S(1)}, s32[3]{0:T(128)}, u32[]{:S(2)}) copy-start(s32[3]{0:T(128)} %param.12) | copy-start | bytes 40
  51.7 22.2 %all-to-all-start.2 = ((bf16[4,768,256]{2,1,0:T(8,128)(2,1)}), bf16[4,768,256]{2,1,0:T(8,128)(2,1)S(1)}, u32[]{:S(2)}, u32[]{:S(2)}) async-start(bf16[4,768,256]{2,1,0:T(8,128)(2,1)} %arrange.1), calls=%async_computation.2 | async-start | bytes 3145728 | tf_op jit(solution)/shard_map/all_to_all | solution.py:237
Sparse Core Ops, SparseCore 0:
  11.0 66.2 all-gather.1
